TPU v7x, 512 devices: a whole 4x8x8 slice. The times are simulated.
512 devices in a mesh: dp: 64 (over z, x, core), tensor: 8 (over y).
Axes of the slice: x: 4, y: 8, z: 8, core: 2. Of those that a mesh axis runs over, the one named last changes fastest.
Arguments:
- gradients: bfloat16 [8, 512, 256, 256], P(None, 'tensor', 'dp')
- owners: int32 [512], P('tensor'), may hold values from 0 to 63, as said below
- left_stats: float32 [1024, 256, 256], P(('dp', 'tensor')), as said below
- right_stats: float32 [1024, 256, 256], P(('dp', 'tensor')), as said below
- left_roots: bfloat16 [1024, 256, 256], P(('dp', 'tensor')), as said below
- right_roots: bfloat16 [1024, 256, 256], P(('dp', 'tensor')), as said below
Outputs:
- preconditioned: bfloat16 [8, 512, 256, 256], P(None, 'tensor', 'dp')
- left_updated: float32 [1024, 256, 256], P(('dp', 'tensor'))
- right_updated: float32 [1024, 256, 256], P(('dp', 'tensor'))
Inputs may be any that keep to these rules, and one draw needn't show every extreme that they name: Each tensor shard's 64 blocks name dp indices as owners; no index is named by more than 2 blocks of one shard, and in every shard some index is named by exactly 2. `left_stats`: every slot's matrix is symmetric. `right_stats`: every slot's matrix is symmetric. `left_roots`: every slot's matrix is symmetric. `right_roots`: every slot's matrix is symmetric.
All inputs are finite; a program needn't handle non-finite values.
Results may differ from a plain program's by a relative error of at most 0.0049.
Values may be sent and summed in bfloat16 or wider, within the bound.
A program may use at most 64 MiB of HBM per device.

v0:
```python
import jax
import jax.numpy as jnp
from jax import lax
from jax.sharding import PartitionSpec as P

SECOND_MOMENT = 0.95
CLIP_EPSILON = 1e-06
GRAFT_EPSILON = 1e-06


def slot_numbers(owner_row):
    block_count = owner_row.shape[0]
    position = jnp.arange(block_count, dtype=jnp.int32)
    same_owner = owner_row[:, None] == owner_row[None, :]
    earlier = position[None, :] < position[:, None]
    return jnp.sum((same_owner & earlier).astype(jnp.int32), axis=1)


def update_slots(
    gradient, clip_value, left_gram, right_gram, left_roots, right_roots, block_square
):
    block_width = gradient.shape[-1]
    weight = (1.0 - SECOND_MOMENT) * clip_value * clip_value / block_width
    left_gram = SECOND_MOMENT * left_gram + weight * jnp.einsum(
        "kij,klj->kil", gradient, gradient, preferred_element_type=jnp.float32
    )
    right_gram = SECOND_MOMENT * right_gram + weight * jnp.einsum(
        "kji,kjl->kil", gradient, gradient, preferred_element_type=jnp.float32
    )
    left_part = jnp.einsum(
        "kij,kjl->kil", left_roots, gradient, preferred_element_type=jnp.float32
    ).astype(jnp.bfloat16)
    direction = jnp.einsum(
        "kij,kjl->kil", left_part, right_roots, preferred_element_type=jnp.float32
    )
    gradient_mean = block_square / (block_width * block_width)
    direction_mean = jnp.mean(direction * direction, axis=(1, 2))
    graft_ratio = clip_value * jnp.sqrt(gradient_mean) / jnp.sqrt(direction_mean + GRAFT_EPSILON)
    return ((graft_ratio[:, None, None] * direction).astype(jnp.bfloat16), left_gram, right_gram)


def shards(gradients, owners, left_stats, right_stats, left_roots, right_roots):
    step_count, block_count, piece_rows, block_width = gradients.shape
    holders = lax.axis_size("dp")
    devices = holders * lax.axis_size("tensor")
    capacity = left_stats.shape[0]
    slot_index = slot_numbers(owners)
    position = jnp.arange(block_count, dtype=jnp.int32)
    pair_index = jnp.arange(capacity * holders, dtype=jnp.int32)
    matches = (owners[None, :] == (pair_index % holders)[:, None]) & (
        slot_index[None, :] == (pair_index // holders)[:, None]
    )
    present = jnp.any(matches, axis=1)
    source = jnp.sum(jnp.where(matches, position[None, :], 0), axis=1)
    home_index = slot_index * holders + owners
    my_owner = lax.axis_index("dp")
    capacity_range = jnp.arange(capacity, dtype=jnp.int32)
    live_slots = jnp.any(
        (owners[None, :] == my_owner) & (slot_index[None, :] == capacity_range[:, None]), axis=1
    )
    picked = jnp.take(gradients, source, axis=-3)
    picked = jnp.where(present[:, None, None], picked, jnp.zeros((), gradients.dtype))
    arrived = lax.all_to_all(
        picked.reshape(gradients.shape[:-3] + (capacity, holders, piece_rows, block_width)),
        "dp",
        split_axis=2,
        concat_axis=2,
        tiled=True,
    )
    received = [
        arrived[moment].reshape(capacity, block_width, block_width) for moment in range(step_count)
    ]
    block_square = [
        jnp.sum(jnp.square(piece.astype(jnp.float32)), axis=(1, 2)) for piece in received
    ]
    total_count = devices * block_count * piece_rows * block_width
    local_sum = jnp.sum(jnp.square(gradients.astype(jnp.float32)), axis=(1, 2, 3))
    totals = lax.psum(local_sum, ("dp", "tensor"))
    clip_factor = jnp.minimum(1.0, 1.0 / jnp.sqrt(totals / total_count + CLIP_EPSILON))
    left_gram = left_stats
    right_gram = right_stats
    outputs = []
    for moment in range(step_count):
        result, left_gram, right_gram = update_slots(
            received[moment],
            clip_factor[moment],
            left_gram,
            right_gram,
            left_roots,
            right_roots,
            block_square[moment],
        )
        outputs.append(result)
    keep_slot = live_slots[:, None, None]
    left_updated = jnp.where(keep_slot, left_gram, left_stats)
    right_updated = jnp.where(keep_slot, right_gram, right_stats)
    outgoing = jnp.stack(outputs).reshape(step_count, capacity, holders, piece_rows, block_width)
    returned = lax.all_to_all(outgoing, "dp", split_axis=2, concat_axis=2, tiled=True).reshape(
        step_count, capacity * holders, piece_rows, block_width
    )
    preconditioned = jnp.take(returned, home_index, axis=1)
    return (preconditioned, left_updated, right_updated)


def solution(mesh):
    in_specs = (
        P(None, "tensor", "dp", None),
        P("tensor"),
        P(("dp", "tensor"), None, None),
        P(("dp", "tensor"), None, None),
        P(("dp", "tensor"), None, None),
        P(("dp", "tensor"), None, None),
    )
    out_specs = (
        P(None, "tensor", "dp", None),
        P(("dp", "tensor"), None, None),
        P(("dp", "tensor"), None, None),
    )
    return jax.shard_map(shards, mesh=mesh, in_specs=in_specs, out_specs=out_specs, check_vma=False)
```

profile of v0, /device:TPU:1, one launch (start us, length us, event | category | flops | bytes accessed | tf_op | source)
XLA Modules:
  0.0 288.7 jit_solution(11884318979202151053)
XLA Ops:
  3.3 3.9 %gather_fusion = bf16[128,8,4,256]{3,2,1,0:T(4,128)(2,1)S(1)} fusion(bf16[8,64,4,256]{3,2,1,0:T(4,128)(2,1)} %param.6, s32[1024]{0:T(1024)S(1)} %pad_clamp_fusion.1), kind=kCustom, calls=%fused_computation | custom fusion | bytes 4194816 | tf_op jit(solution)/shard_map/jit(_take)/gather | solution.py:61
  8.8 3.0 %copy.217 = bf16[8,2,64,4,256]{4,3,1,0,2:T(4,128)(2,1)} copy(bf16[8,2,64,4,256]{4,2,1,3,0:T(8,128)(2,1)S(1)} %select_select_fusion) | data formatting | bytes 4194304 | tf_op jit(solution)/shard_map/jit(_where)/select_n | solution.py:62
  11.7 15.0 %all-to-all-start = ((bf16[8,2,64,4,256]{4,3,1,0,2:T(4,128)(2,1)}), bf16[8,2,64,4,256]{4,3,1,0,2:T(4,128)(2,1)S(1)}, u32[]{:S(2)}, u32[]{:S(2)}) async-start(bf16[8,2,64,4,256]{4,3,1,0,2:T(4,128)(2,1)} %copy.217), calls=%async_computation | async-start | bytes 4194304 | tf_op jit(solution)/shard_map/all_to_all | solution.py:63
  27.4 136.4 %psum.7 = f32[8]{0:T(128)S(1)} all-reduce(f32[8]{0:T(128)S(1)} %multiply_reduce_fusion), channel_id=1, replica_groups=mesh['dp'=64,'tensor'=8] {'dp','tensor'}, use_global_device_ids=true, to_apply=%region_2.3 | all-reduce | flops 8 | bytes 64 | tf_op jit(solution)/shard_map/psum | solution.py:78
  174.4 1.6 fusion.59
  181.4 1.9 copy.227
  183.3 1.8 copy.228
  185.1 1.9 copy.224
  187.0 1.8 copy.225
  188.8 1.8 copy.221
  190.6 1.8 copy.222
  192.4 1.9 copy.218
  194.3 1.8 copy.219
  196.1 2.3 multiply_reduce_fusion.1
  200.4 1.6 multiply_reduce_fusion.3
  209.5 1.7 stack.30
  213.3 1.7 stack.29
  222.1 2.5 copy.292
  224.6 8.7 %all-to-all-start.1 = ((bf16[8,2,64,4,256]{4,3,1,0,2:T(4,128)(2,1)}), bf16[8,2,64,4,256]{4,3,1,0,2:T(4,128)(2,1)S(1)}, u32[]{:S(2)}, u32[]{:S(2)}) async-start(bf16[8,2,64,4,256]{4,3,1,0,2:T(4,128)(2,1)} %copy.292), calls=%async_computation.1 | async-start | bytes 4194304 | tf_op jit(solution)/shard_map/all_to_all | solution.py:98
  233.4 1.5 fusion.31
  242.5 40.5 %all-to-all-done.1 = bf16[8,2,64,4,256]{4,3,1,0,2:T(4,128)(2,1)S(1)} async-done(((bf16[8,2,64,4,256]{4,3,1,0,2:T(4,128)(2,1)}), bf16[8,2,64,4,256]{4,3,1,0,2:T(4,128)(2,1)S(1)}, u32[]{:S(2)}, u32[]{:S(2)}) %all-to-all-start.1) | async-done | bytes 2097184 | tf_op jit(solution)/shard_map/all_to_all | solution.py:98
  283.0 1.9 copy.250
  285.0 2.2 gather_fusion.1
  287.3 1.4 copy.283
  (137 shorter events, 37.2 us)
Async XLA Ops:
  0.6 195.5 %copy-start = (bf16[2,256,256]{2,1,0:T(8,128)(2,1)S(1)}, bf16[2,256,256]{2,1,0:T(8,128)(2,1)}, u32[]{:S(2)}) copy-start(bf16[2,256,256]{2,1,0:T(8,128)(2,1)} %param.11) | copy-start | bytes 786436
  11.7 15.0 %copy-start.2 = (bf16[8,64,4,256]{3,2,1,0:T(4,128)(2,1)S(1)}, bf16[8,64,4,256]{3,2,1,0:T(4,128)(2,1)}, u32[]{:S(2)}) copy-start(bf16[8,64,4,256]{3,2,1,0:T(4,128)(2,1)} %param.6) | copy-start | bytes 3145732
  11.7 162.5 %copy-start.28 = (s32[64]{0:T(128)S(1)}, s32[64]{0:T(128)}, u32[]{:S(2)}) copy-start(s32[64]{0:T(128)} %param.7) | copy-start | bytes 772
  11.7 162.6 %all-to-all-start = ((bf16[8,2,64,4,256]{4,3,1,0,2:T(4,128)(2,1)}), bf16[8,2,64,4,256]{4,3,1,0,2:T(4,128)(2,1)S(1)}, u32[]{:S(2)}, u32[]{:S(2)}) async-start(bf16[8,2,64,4,256]{4,3,1,0,2:T(4,128)(2,1)} %copy.217), calls=%async_computation | async-start | bytes 4194304 | tf_op jit(solution)/shard_map/all_to_all | solution.py:63
  176.2 5.2 %copy-start.7 = (bf16[1,2,64,4,256]{4,1,3,2,0:T(2,128)(2,1)}, bf16[1,2,64,4,256]{4,1,3,2,0:T(2,128)(2,1)S(1)}, u32[]{:S(2)}) copy-start(bf16[1,2,64,4,256]{4,1,3,2,0:T(2,128)(2,1)S(1)} %copy.239) | copy-start | bytes 786436
  181.4 14.7 %copy-start.1 = (bf16[2,256,256]{2,1,0:T(8,128)(2,1)S(1)}, bf16[2,256,256]{2,1,0:T(8,128)(2,1)}, u32[]{:S(2)}) copy-start(bf16[2,256,256]{2,1,0:T(8,128)(2,1)} %param.10) | copy-start | bytes 786436
  198.4 1.9 copy-start.24
  199.6 3.3 %copy-start.10 = (bf16[2,256,256]{1,2,0:T(8,128)(2,1)S(1)}, bf16[2,256,256]{1,2,0:T(8,128)(2,1)}, u32[]{:S(2)}) copy-start(bf16[2,256,256]{1,2,0:T(8,128)(2,1)} %copy.234) | copy-start | bytes 786436
  202.0 2.3 copy-start.12
  203.5 3.9 %copy-start.14 = (bf16[2,256,256]{1,2,0:T(8,128)(2,1)S(1)}, bf16[2,256,256]{1,2,0:T(8,128)(2,1)}, u32[]{:S(2)}) copy-start(bf16[2,256,256]{1,2,0:T(8,128)(2,1)} %copy.228) | copy-start | bytes 786436
  204.9 6.3 %copy-start.16 = (bf16[2,256,256]{1,2,0:T(8,128)(2,1)S(1)}, bf16[2,256,256]{1,2,0:T(8,128)(2,1)}, u32[]{:S(2)}) copy-start(bf16[2,256,256]{1,2,0:T(8,128)(2,1)} %copy.225) | copy-start | bytes 786436
  208.0 7.0 %copy-start.18 = (bf16[2,256,256]{1,2,0:T(8,128)(2,1)S(1)}, bf16[2,256,256]{1,2,0:T(8,128)(2,1)}, u32[]{:S(2)}) copy-start(bf16[2,256,256]{1,2,0:T(8,128)(2,1)} %copy.222) | copy-start | bytes 786436
  211.8 5.3 %copy-start.20 = (bf16[2,256,256]{1,2,0:T(8,128)(2,1)S(1)}, bf16[2,256,256]{1,2,0:T(8,128)(2,1)}, u32[]{:S(2)}) copy-start(bf16[2,256,256]{1,2,0:T(8,128)(2,1)} %copy.219) | copy-start | bytes 786436
  217.1 4.4 %copy-start.26 = (bf16[1,2,64,4,256]{4,3,2,1,0:T(4,128)(2,1)S(1)}, bf16[1,2,64,4,256]{4,3,2,1,0:T(4,128)(2,1)}, u32[]{:S(2)}) copy-start(bf16[1,2,64,4,256]{4,3,2,1,0:T(4,128)(2,1)} %stack.30) | copy-start | bytes 786436
  217.7 3.7 %copy-start.27 = (bf16[1,2,64,4,256]{4,3,2,1,0:T(4,128)(2,1)S(1)}, bf16[1,2,64,4,256]{4,3,2,1,0:T(4,128)(2,1)}, u32[]{:S(2)}) copy-start(bf16[1,2,64,4,256]{4,3,2,1,0:T(4,128)(2,1)} %stack.29) | copy-start | bytes 786436
  224.6 58.4 %all-to-all-start.1 = ((bf16[8,2,64,4,256]{4,3,1,0,2:T(4,128)(2,1)}), bf16[8,2,64,4,256]{4,3,1,0,2:T(4,128)(2,1)S(1)}, u32[]{:S(2)}, u32[]{:S(2)}) async-start(bf16[8,2,64,4,256]{4,3,1,0,2:T(4,128)(2,1)} %copy.292), calls=%async_computation.1 | async-start | bytes 4194304 | tf_op jit(solution)/shard_map/all_to_all | solution.py:98
  233.3 2.9 copy-start.4
  233.4 3.1 %copy-start.3 = (bf16[1,2,64,4,256]{4,1,3,2,0:T(2,128)(2,1)S(1)}, bf16[1,2,64,4,256]{4,1,3,2,0:T(2,128)(2,1)}, u32[]{:S(2)}) copy-start(bf16[1,2,64,4,256]{4,1,3,2,0:T(2,128)(2,1)} %copy.227) | copy-start | bytes 786436
  236.8 1.2 copy-start.25
  237.1 1.2 copy-start.5
  237.1 1.2 copy-start.19
  237.4 1.1 copy-start.17
  239.3 1.1 copy-start.23
  240.0 1.5 copy-start.22
  (7 other events, 7.0 us)
where the time goes:
time: 291 us; the launch traced here: 289 us
  blocking collectives  136 us (47%)
  local copies, waits for them, and re-layouts  48 us (16%)
  waiting for transfers between devices  40.5 us (14%)
  starting transfers between devices  23.7 us (8%)
  matrix products  15.3 us (5%)
  other arithmetic  13.9 us (5%)
  between operations  10.9 us (4%)
    psum x1, blocking collectives, shards(): totals = lax.psum(local_sum, ('dp', 'tensor'))  136 us
    all_to_all x1, waiting for transfers between devices, shards(): lax.all_to_all(outgoing, 'dp', split_axis=2, concat_axis=2, tiled=True)  40.5 us
    all_to_all x1, starting transfers between devices, shards(): lax.all_to_all(picked.reshape(gradients.shape[:-3] + (capacity, holders,...  15 us
    slice x9, local copies, waits for them, and re-layouts, shards(): arrived[moment].reshape(capacity, block_width, block_width)  10.9 us
    another operation x8, local copies, waits for them, and re-layouts, shards(): arrived[moment].reshape(capacity, block_width, block_width)  10.8 us
    another operation x10, local copies, waits for them, and re-layouts, shards(): jnp.stack(outputs)  9.05 us
    all_to_all x1, starting transfers between devices, shards(): lax.all_to_all(outgoing, 'dp', split_axis=2, concat_axis=2, tiled=True)  8.72 us
    dot_general x8, matrix products, update_slots(): jnp.einsum('kij,kjl->kil', left_part, right_roots, preferred_element_type...  7.42 us
  transfers between devices with their start and end apart: 2, of which 1 were waited for; matrix products, arithmetic and copies ran while one was open for 3% of the time, Pallas kernels for 0%

commit v1 on v0

v1 whole, which is shorter than its diff:
```python
import functools

import jax
import jax.numpy as jnp
from jax import lax
from jax.experimental import pallas as pl
from jax.experimental.pallas import tpu as pltpu
from jax.sharding import PartitionSpec as P

SECOND_MOMENT = 0.95
CLIP_EPSILON = 1e-06
GRAFT_EPSILON = 1e-06
MESH = pl.DeviceIdType.MESH

CHUNKS = 2
TILE_ROWS, TILE_COLS = 16, 128


def routes(owners):
    count = owners.shape[0]
    position = jnp.arange(count, dtype=jnp.int32)
    same_owner = owners[:, None] == owners[None, :]
    earlier = position[None, :] < position[:, None]
    slot = jnp.sum((same_owner & earlier).astype(jnp.int32), axis=1)
    owned = owners[None, :] == position[:, None]
    first = owned & (slot == 0)[None, :]
    second = owned & (slot == 1)[None, :]
    has_first = jnp.any(first, axis=1)
    has_second = jnp.any(second, axis=1)
    first_block = jnp.sum(jnp.where(first, position[None, :], 0), axis=1)
    second_block = jnp.sum(jnp.where(second, position[None, :], 0), axis=1)
    before = position[None, :] < position[:, None]
    empty_rank = jnp.sum((before & ~has_first[None, :]).astype(jnp.int32), axis=1)
    second_rank = jnp.sum((before & has_second[None, :]).astype(jnp.int32), axis=1)
    match = (
        (empty_rank[:, None] == second_rank[None, :])
        & ~has_first[:, None]
        & has_second[None, :]
    )
    helped = jnp.sum(jnp.where(match, position[None, :], 0), axis=1)
    helper = jnp.sum(jnp.where(match, position[:, None], 0), axis=0)
    helped_block = jnp.sum(jnp.where(match, second_block[None, :], 0), axis=1)
    block_of = jnp.where(has_first, first_block, helped_block)
    device_of = jnp.sum(
        jnp.where(block_of[:, None] == position[None, :], position[:, None], 0), axis=0
    )
    return jnp.stack(
        [
            block_of,
            device_of,
            helped,
            helper,
            has_first.astype(jnp.int32),
            has_second.astype(jnp.int32),
        ]
    )


def kernel(
    sizes,
    table,
    x_ref,
    left_stats,
    right_stats,
    left_roots,
    right_roots,
    y_ref,
    left_out,
    right_out,
    byblock,
    stage,
    land,
    grads,
    outs,
    back_stage,
    back_first,
    back_second,
    roots_a,
    roots_b,
    roots_c,
    roots_d,
    grams_a,
    grams_b,
    grams_c,
    grams_d,
    root_use,
    gram_sum,
    sums_y,
    sums_dp,
    send_y,
    recv_y,
    send_dp,
    recv_dp,
    send_tile,
    recv_tile,
    send_go,
    recv_go,
    send_back,
    recv_back,
):
    steps, holders, shards, piece, width, total_count = sizes
    back = (back_first, back_second)
    chunk_steps = steps // CHUNKS
    rows = piece * chunk_steps
    group = width // rows
    groups = holders // group
    span = group * piece
    me = lax.axis_index("dp")
    shard = lax.axis_index("tensor")

    def peer(k):
        return lax.rem(me + k, holders)

    barrier = pltpu.get_barrier_semaphore()

    def greet(k, carry):
        pl.semaphore_signal(barrier, inc=1, device_id=(peer(k), shard), device_id_type=MESH)
        return carry

    def greet_shard(k, carry):
        pl.semaphore_signal(
            barrier, inc=1, device_id=(me, lax.rem(shard + k, shards)), device_id_type=MESH
        )
        return carry

    lax.fori_loop(1, shards, greet_shard, 0)
    lax.fori_loop(1, holders, greet, 0)

    lane = lax.broadcasted_iota(jnp.int32, (1, TILE_COLS), 1)

    def add_square(s, row):
        values = x_ref[s].astype(jnp.float32)
        square = jnp.sum(values * values, axis=(0, 1), keepdims=True)
        return row + jnp.where(lane == s, square, 0.0)

    local_row = lax.fori_loop(0, steps, add_square, jnp.zeros((1, TILE_COLS), jnp.float32))
    sums_y[pl.ds(shard, 1)] = local_row[None]

    out_index = lax.broadcasted_iota(jnp.int32, (width, width), 0)
    in_index = lax.broadcasted_iota(jnp.int32, (width, width), 1)

    def by_device(index):
        step, rest = index // span, index % span
        return (rest // piece) * rows + step * piece + rest % piece

    apart = (out_index == by_device(in_index)).astype(jnp.bfloat16)
    together = (by_device(out_index) == in_index).astype(jnp.bfloat16)

    def permute(matrix, values):
        return jnp.dot(matrix, values, preferred_element_type=jnp.float32).astype(jnp.bfloat16)

    def split_by_device(c, g, source, target):
        part = source[pl.ds(c * chunk_steps, chunk_steps), pl.ds(g * span, span), :]
        done = permute(apart, part.reshape(width, width))
        target[c, pl.ds(g * group, group)] = done.reshape(group, rows, width)

    def prepare(i, carry):
        split_by_device(i // groups, i % groups, x_ref, byblock)
        return carry

    lax.fori_loop(0, CHUNKS * groups, prepare, 0)

    row_tiles, col_tiles = width // TILE_ROWS, width // TILE_COLS

    def tiles_of(matrix, target, base):
        for i in range(row_tiles):
            for j in range(col_tiles):
                target[base + i * col_tiles + j] = matrix[
                    i * TILE_ROWS : (i + 1) * TILE_ROWS, j * TILE_COLS : (j + 1) * TILE_COLS
                ]

    def matrix_of(source, base):
        return jnp.concatenate(
            [
                jnp.concatenate([source[base + i * col_tiles + j] for j in range(col_tiles)], axis=1)
                for i in range(row_tiles)
            ],
            axis=0,
        )

    half = row_tiles * col_tiles
    tiles_of(left_roots[1], roots_a, 0)
    tiles_of(right_roots[1], roots_a, half)

    pl.semaphore_wait(barrier, holders - 1 + shards - 1)

    def copy(source, target, send, recv, device, t=None):
        return pltpu.make_async_remote_copy(
            src_ref=source,
            dst_ref=target,
            send_sem=send,
            recv_sem=recv,
            device_id=(device, shard if t is None else t),
            device_id_type=MESH,
        )

    def wait_bytes(ref, count, semaphore):
        part = ref.at[pl.ds(0, count)]
        pltpu.make_async_copy(part, part, semaphore).wait()

    def send_shard(k, carry):
        t = lax.rem(shard + k, shards)
        copy(sums_y.at[shard], sums_y.at[shard], send_y, recv_y, me, t).start()
        return carry

    lax.fori_loop(1, shards, send_shard, 0)

    def send_tiles(source, target, which):
        def one(k, carry):
            d = peer(k)
            copy(
                source.at[d], target.at[me], send_tile.at[which], recv_tile.at[which], d
            ).start()
            return carry

        lax.fori_loop(1, holders, one, 0)
        target[pl.ds(me, 1)] = source[pl.ds(me, 1)]

    def pass_tiles(source, staged, target, which, row):
        def one(k, carry):
            d = peer(k)
            staged[d] = source[table[row, d]]
            copy(
                staged.at[d], target.at[me], send_tile.at[which], recv_tile.at[which], d
            ).start()
            return carry

        lax.fori_loop(1, holders, one, 0)
        target[me] = source[table[row, me]]

    send_tiles(roots_a, roots_b, 0)

    def send_gradients(c):
        def one(k, carry):
            d = peer(k)
            stage[c, d] = byblock[c, table[0, d]]
            copy(stage.at[c, d], land.at[c, me], send_go.at[c], recv_go.at[c], d).start()
            return carry

        lax.fori_loop(1, holders, one, 0)
        land[c, me] = byblock[c, table[0, me]]

    send_gradients(0)

    wait_bytes(sums_y, shards - 1, recv_y)
    shard_row = sums_y[0]
    for t in range(1, shards):
        shard_row = shard_row + sums_y[t]
    sums_dp[pl.ds(me, 1)] = shard_row[None]

    def send_sums(k, carry):
        d = peer(k)
        copy(sums_dp.at[me], sums_dp.at[me], send_dp, recv_dp, d).start()
        return carry

    lax.fori_loop(1, holders, send_sums, 0)

    wait_bytes(roots_b, holders - 1, recv_tile.at[0])
    pass_tiles(roots_b, roots_c, roots_d, 1, 2)

    for c in range(1, CHUNKS):
        send_gradients(c)

    wait_bytes(sums_dp, holders - 1, recv_dp)
    totals = jnp.sum(sums_dp[...], axis=0)
    clip_row = jnp.minimum(1.0, 1.0 / jnp.sqrt(totals / total_count + CLIP_EPSILON))

    def clip_of(s):
        return jnp.sum(jnp.where(lane == s, clip_row, 0.0), axis=1, keepdims=True)

    has_first = table[4, me]
    has_second = table[5, me]

    def gather_steps(c):
        wait_bytes(land.at[c], holders - 1, recv_go.at[c])

        def one(g, carry):
            values = land[c, pl.ds(g * group, group)].reshape(width, width)
            done = permute(together, values).reshape(chunk_steps, span, width)
            grads[pl.ds(c * chunk_steps, chunk_steps), pl.ds(g * span, span), :] = done
            return carry

        lax.fori_loop(0, groups, one, 0)

    def directions(c):
        def one(s, carry):
            gradient = grads[s]
            wide = gradient.astype(jnp.float32)
            square = jnp.sum(wide * wide, axis=(0, 1), keepdims=True)
            left_part = jnp.dot(
                root_use[0], gradient, preferred_element_type=jnp.float32
            ).astype(jnp.bfloat16)
            direction = jnp.dot(left_part, root_use[1], preferred_element_type=jnp.float32)
            direction_square = jnp.sum(direction * direction, axis=(0, 1), keepdims=True)
            area = float(width * width)
            ratio = (
                clip_of(s)
                * jnp.sqrt(square / area)
                / jnp.sqrt(direction_square / area + GRAFT_EPSILON)
            )
            outs[s] = (ratio * direction).astype(jnp.bfloat16)
            return carry

        lax.fori_loop(c * chunk_steps, (c + 1) * chunk_steps, one, 0)

        def sort(g, carry):
            split_by_device(c, g, outs, back_stage)
            return carry

        lax.fori_loop(0, groups, sort, 0)

        def send(k, carry):
            d = peer(k)
            copy(
                back_stage.at[c, d], back[c].at[me], send_back.at[c], recv_back.at[c], d
            ).start()
            return carry

        lax.fori_loop(1, holders, send, 0)
        back[c][me] = back_stage[c, me]

    gather_steps(0)
    wait_bytes(roots_d, holders - 1, recv_tile.at[1])
    root_use[0] = jnp.where(has_first > 0, left_roots[0], matrix_of(roots_d, 0))
    root_use[1] = jnp.where(has_first > 0, right_roots[0], matrix_of(roots_d, half))
    for c in range(CHUNKS - 1):
        directions(c)
        gather_steps(c + 1)

    gram_sum[...] = jnp.zeros_like(gram_sum)

    def add_gram(s, carry):
        gradient = grads[s]
        clip = clip_of(s)
        weight = (1.0 - SECOND_MOMENT) * clip * clip / width
        left = lax.dot_general(
            gradient, gradient, (((1,), (1,)), ((), ())), preferred_element_type=jnp.float32
        )
        right = lax.dot_general(
            gradient, gradient, (((0,), (0,)), ((), ())), preferred_element_type=jnp.float32
        )
        gram_sum[0] = SECOND_MOMENT * gram_sum[0] + weight * left
        gram_sum[1] = SECOND_MOMENT * gram_sum[1] + weight * right
        return carry

    lax.fori_loop(0, steps, add_gram, 0)
    tiles_of(gram_sum[0].astype(jnp.bfloat16), grams_a, 0)
    tiles_of(gram_sum[1].astype(jnp.bfloat16), grams_a, half)
    send_tiles(grams_a, grams_b, 2)
    directions(CHUNKS - 1)

    kept = SECOND_MOMENT**steps
    left_out[0] = jnp.where(has_first > 0, kept * left_stats[0] + gram_sum[0], left_stats[0])
    right_out[0] = jnp.where(has_first > 0, kept * right_stats[0] + gram_sum[1], right_stats[0])

    wait_bytes(grams_b, holders - 1, recv_tile.at[2])
    pass_tiles(grams_b, grams_c, grams_d, 3, 3)

    def finish(c):
        wait_bytes(back[c], holders - 1, recv_back.at[c])

        def one(g, carry):
            values = jnp.concatenate(
                [back[c][table[1, g * group + i]] for i in range(group)], axis=0
            )
            done = permute(together, values).reshape(chunk_steps, span, width)
            y_ref[pl.ds(c * chunk_steps, chunk_steps), pl.ds(g * span, span), :] = done
            return carry

        lax.fori_loop(0, groups, one, 0)

    for c in range(CHUNKS):
        finish(c)

    wait_bytes(grams_d, holders - 1, recv_tile.at[3])
    left_new = kept * left_stats[1] + matrix_of(grams_d, 0).astype(jnp.float32)
    right_new = kept * right_stats[1] + matrix_of(grams_d, half).astype(jnp.float32)
    left_out[1] = jnp.where(has_second > 0, left_new, left_stats[1])
    right_out[1] = jnp.where(has_second > 0, right_new, right_stats[1])

    wait_bytes(sums_y, shards - 1, send_y)
    wait_bytes(sums_dp, holders - 1, send_dp)
    for which in range(4):
        wait_bytes(roots_a, holders - 1, send_tile.at[which])
    for c in range(CHUNKS):
        wait_bytes(stage.at[c], holders - 1, send_go.at[c])
        wait_bytes(back_stage.at[c], holders - 1, send_back.at[c])


def shards_step(gradients, owners, left_stats, right_stats, left_roots, right_roots):
    steps, blocks, piece, width = gradients.shape
    holders = lax.axis_size("dp")
    shards = lax.axis_size("tensor")
    rows = piece * (steps // CHUNKS)
    total_count = float(holders * shards * blocks * piece * width)
    table = routes(owners)
    bf16, f32 = jnp.bfloat16, jnp.float32
    message = pltpu.VMEM((CHUNKS, blocks, rows, width), bf16)
    arrivals = pltpu.VMEM((blocks, rows, width), bf16)
    by_step = pltpu.VMEM((steps, width, width), bf16)
    tiles = pltpu.VMEM((holders, TILE_ROWS, TILE_COLS), bf16)
    dma = pltpu.SemaphoreType.DMA
    vmem = pl.BlockSpec(memory_space=pltpu.VMEM)
    sizes = (steps, holders, shards, piece, width, total_count)
    y, left, right = pl.pallas_call(
        functools.partial(kernel, sizes),
        name="shampoo",
        out_shape=(
            jax.ShapeDtypeStruct((steps, blocks * piece, width), bf16),
            jax.ShapeDtypeStruct(left_stats.shape, f32),
            jax.ShapeDtypeStruct(right_stats.shape, f32),
        ),
        in_specs=[pl.BlockSpec(memory_space=pltpu.SMEM)] + [vmem] * 5,
        out_specs=(vmem,) * 3,
        scratch_shapes=[
            message,
            message,
            message,
            by_step,
            by_step,
            message,
            arrivals,
            arrivals,
            tiles,
            tiles,
            tiles,
            tiles,
            tiles,
            tiles,
            tiles,
            tiles,
            pltpu.VMEM((2, width, width), bf16),
            pltpu.VMEM((2, width, width), f32),
            pltpu.VMEM((shards, 1, TILE_COLS), f32),
            pltpu.VMEM((holders, 1, TILE_COLS), f32),
            dma,
            dma,
            dma,
            dma,
            dma((4,)),
            dma((4,)),
            dma((CHUNKS,)),
            dma((CHUNKS,)),
            dma((CHUNKS,)),
            dma((CHUNKS,)),
        ],
        compiler_params=pltpu.CompilerParams(
            collective_id=0, has_side_effects=True, vmem_limit_bytes=40 << 20
        ),
    )(
        table,
        gradients.reshape(steps, blocks * piece, width),
        left_stats,
        right_stats,
        left_roots,
        right_roots,
    )
    return y.reshape(gradients.shape), left, right


def solution(mesh):
    in_specs = (
        P(None, "tensor", "dp", None),
        P("tensor"),
        P(("dp", "tensor"), None, None),
        P(("dp", "tensor"), None, None),
        P(("dp", "tensor"), None, None),
        P(("dp", "tensor"), None, None),
    )
    out_specs = (
        P(None, "tensor", "dp", None),
        P(("dp", "tensor"), None, None),
        P(("dp", "tensor"), None, None),
    )
    return jax.shard_map(
        shards_step, mesh=mesh, in_specs=in_specs, out_specs=out_specs, check_vma=False
    )
```

time: 291 us -> 97.7 us (0.34)
  blocking collectives: 136 us -> 0 us
  Pallas kernels: 0 us -> 87.2 us
  waiting for transfers between devices: 40.5 us -> 0 us
  local copies, waits for them, and re-layouts: 48 us -> 7.86 us
  starting transfers between devices: 23.7 us -> 0 us
  matrix products: 15.3 us -> 0 us
  other arithmetic: 13.9 us -> 1.6 us
  between operations: 10.9 us -> 0.73 us
    psum x1 -> x0, blocking collectives: 136 us -> none  [shards(): totals = lax.psum(local_sum, ('dp', 'tensor'))]
    pallas_call x0 -> x1, Pallas kernels: none -> 87.2 us  [shards_step(): pl.pallas_call(functools.partial(kernel, sizes), name='shampoo', out_shap...]
    all_to_all x2 -> x0, waiting for transfers between devices: 40.5 us -> none  [the longest x1 40.5 us: shards(): lax.all_to_all(outgoing, 'dp', split_axis=2, concat_axis=2, tiled=True)]
    all_to_all x2 -> x0, starting transfers between devices: 23.7 us -> none  [the longest x1 15 us: shards(): lax.all_to_all(picked.reshape(gradients.shape[:-3] + (capacity, holders,...]
    another operation x18 -> x1, local copies, waits for them, and re-layouts: 19.9 us -> 0.03 us  [routes(): jnp.stack([block_of, device_of, helped, helper, has_first.astype(jnp.int3...]
    dot_general x24 -> x0, matrix products: 15.3 us -> none  [the longest x8 7.42 us: update_slots(): jnp.einsum('kij,kjl->kil', left_part, right_roots, preferred_element_type...]
    slice x10 -> x0, local copies, waits for them, and re-layouts: 11.5 us -> none  [the longest x9 10.9 us: shards(): arrived[moment].reshape(capacity, block_width, block_width)]
    gather x3 -> x0, local copies, waits for them, and re-layouts: 7.32 us -> none  [the longest x2 5.11 us: shards(): picked = jnp.take(gradients, source, axis=-3)]
  transfers between devices with their start and end apart: 2 -> 0, of which waited for: 1 -> 0; matrix products, arithmetic and copies ran while one was open for 3% -> 0% of each run, Pallas kernels for 0% -> 0%
where the time goes in v1:
time: 97.7 us; the launch traced here: 97.4 us
  Pallas kernels  87.2 us (89%)
  local copies, waits for them, and re-layouts  7.86 us (8%)
  other arithmetic  1.6 us (2%)
    pallas_call x1, Pallas kernels, shards_step(): pl.pallas_call(functools.partial(kernel, sizes), name='shampoo', out_shap...  87.2 us
    unnamed x20, local copies, waits for them, and re-layouts  5.31 us

profile of v1, /device:TPU:1, one launch (start us, length us, event | category | flops | bytes accessed | tf_op | source)
XLA Modules:
  0.0 97.4 jit_solution(8196933671703365244)
XLA Ops:
  0.6 0.9 convert_reduce_fusion.2
  1.6 0.0 copy-start.8
  1.6 0.6 copy-done.8
  2.2 0.1 fusion.6
  2.3 0.2 select_reduce_fusion.4
  2.5 0.1 convert_reduce_fusion.1
  2.6 0.2 select_reduce_fusion
  2.8 0.1 select_reduce_fusion.2
  2.9 0.0 copy-start
  3.0 0.0 copy-start.1
  3.0 0.0 copy-start.6
  3.0 1.4 %reshape.73.x_ref = bf16[8,256,256]{2,1,0:T(8,128)(2,1)S(1)} reshape(bf16[8,64,4,256]{3,2,1,0:T(4,128)(2,1)} %param.6) | data formatting | bytes 2097152 | tf_op jit(solution)/shard_map/reshape | solution.py:452
  4.4 0.0 copy-done
  4.4 0.0 copy-done.1
  4.5 0.1 copy-done.6
  4.5 0.9 copy-done.7
  5.5 87.2 %shampoo.1 = (bf16[8,256,256]{2,1,0:T(8,128)(2,1)S(1)}, f32[2,256,256]{2,1,0:T(8,128)S(1)}, f32[2,256,256]{2,1,0:T(8,128)S(1)}) custom-call(s32[6,64]{1,0:T(8,128)S(1)} %stack.18.table, bf16[8,256,256]{2,1,0:T(8,128)(2,1)S(1)} %reshape.73.x_ref, f32[2,256,256]{2,1,0:T(8,128)S(1)} %copy-done, f32[2,256,256]{2,1,0:T(8,128)S(1)} %copy-done.1, ...), custom_call_target="tpu_custom_call" | custom-call | tf_op jit(solution)/shard_map/shampoo/pallas_call | solution.py:405
  92.7 0.0 copy-start.2
  92.7 0.8 copy-done.2
  93.5 0.8 copy-done.4
  94.3 1.1 %reshape.74 = bf16[8,64,4,256]{3,2,1,0:T(4,128)(2,1)} reshape(bf16[8,256,256]{2,1,0:T(8,128)(2,1)S(1)} %get-tuple-element.6) | data formatting | bytes 2097152 | tf_op jit(solution)/shard_map/reshape | solution.py:458
  95.4 0.8 copy.11
  96.2 0.4 copy-done.3
  96.6 0.8 copy.12
  (10 shorter events, 0.1 us)
Async XLA Ops:
  1.6 0.7 copy-start.8
  2.9 1.5 %copy-start = (f32[2,256,256]{2,1,0:T(8,128)S(1)}, f32[2,256,256]{2,1,0:T(8,128)}, u32[]{:S(2)}) copy-start(f32[2,256,256]{2,1,0:T(8,128)} %left_stats.1) | copy-start | bytes 1572868
  3.0 1.5 %copy-start.1 = (f32[2,256,256]{2,1,0:T(8,128)S(1)}, f32[2,256,256]{2,1,0:T(8,128)}, u32[]{:S(2)}) copy-start(f32[2,256,256]{2,1,0:T(8,128)} %right_stats.1) | copy-start | bytes 1572868
  3.0 1.6 %copy-start.6 = (bf16[2,256,256]{2,1,0:T(8,128)(2,1)S(1)}, bf16[2,256,256]{2,1,0:T(8,128)(2,1)}, u32[]{:S(2)}) copy-start(bf16[2,256,256]{2,1,0:T(8,128)(2,1)} %left_roots.1) | copy-start | bytes 786436
  4.5 0.9 copy-start.7
  92.7 0.8 copy-start.2
  93.5 0.8 copy-start.4
  94.3 1.1 %copy-start.5 = (f32[2,256,256]{2,1,0:T(8,128)S(1)}, f32[2,256,256]{2,1,0:T(8,128)}, u32[]{:S(2)}) copy-start(f32[2,256,256]{2,1,0:T(8,128)} %copy-done.4) | copy-start | bytes 1572868
  95.4 1.2 %copy-start.3 = (f32[2,256,256]{2,1,0:T(8,128)S(1)}, f32[2,256,256]{2,1,0:T(8,128)}, u32[]{:S(2)}) copy-start(f32[2,256,256]{2,1,0:T(8,128)} %copy-done.2) | copy-start | bytes 1572868

commit v2 on v1

--- a/solution.py
+++ b/solution.py
@@ -60,13 +60,13 @@
     sizes,
     table,
     x_ref,
-    left_stats,
-    right_stats,
+    left_hbm,
+    right_hbm,
+    y_ref,
+    left_delta,
+    right_delta,
     left_roots,
     right_roots,
-    y_ref,
-    left_out,
-    right_out,
     byblock,
     stage,
     land,
@@ -84,7 +84,6 @@
     grams_c,
     grams_d,
     root_use,
-    gram_sum,
     sums_y,
     sums_dp,
     send_y,
@@ -97,6 +96,7 @@
     recv_go,
     send_back,
     recv_back,
+    load_sem,
 ):
     steps, holders, shards, piece, width, total_count = sizes
     back = (back_first, back_second)
@@ -126,6 +126,13 @@
     lax.fori_loop(1, shards, greet_shard, 0)
     lax.fori_loop(1, holders, greet, 0)
 
+    loads = (
+        pltpu.make_async_copy(left_hbm, left_roots, load_sem.at[0]),
+        pltpu.make_async_copy(right_hbm, right_roots, load_sem.at[1]),
+    )
+    for load in loads:
+        load.start()
+
     lane = lax.broadcasted_iota(jnp.int32, (1, TILE_COLS), 1)
 
     def add_square(s, row):
@@ -160,27 +167,54 @@
 
     lax.fori_loop(0, CHUNKS * groups, prepare, 0)
 
-    row_tiles, col_tiles = width // TILE_ROWS, width // TILE_COLS
-
-    def tiles_of(matrix, target, base):
-        for i in range(row_tiles):
-            for j in range(col_tiles):
-                target[base + i * col_tiles + j] = matrix[
-                    i * TILE_ROWS : (i + 1) * TILE_ROWS, j * TILE_COLS : (j + 1) * TILE_COLS
-                ]
-
-    def matrix_of(source, base):
+    middle = width // 2
+    quarter = middle // TILE_ROWS
+    half = 2 * quarter
+    last = 2 * half
+    down = lax.broadcasted_iota(jnp.int32, (middle, middle), 0)
+    across = lax.broadcasted_iota(jnp.int32, (middle, middle), 1)
+
+    def pack(matrix, target, base):
+        upper_left = matrix[:middle, :middle].astype(jnp.float32)
+        lower_right = matrix[middle:, middle:].astype(jnp.float32)
+        mixed = jnp.where(down >= across, upper_left, lower_right).astype(jnp.bfloat16)
+        below = matrix[middle:, :middle].astype(jnp.bfloat16)
+        target[base : base + quarter] = below.reshape(quarter, TILE_ROWS, middle)
+        target[base + quarter : base + half] = mixed.reshape(quarter, TILE_ROWS, middle)
+        return jnp.sum(jnp.where(down == across, lower_right, 0.0), axis=0, keepdims=True)
+
+    def pack_pair(left, right, target):
+        left_diagonal = pack(left, target, 0)
+        right_diagonal = pack(right, target, half)
+        row = lax.broadcasted_iota(jnp.int32, (TILE_ROWS, middle), 0)
+        target[last] = jnp.where(
+            row == 0, left_diagonal, jnp.where(row == 1, right_diagonal, 0.0)
+        ).astype(jnp.bfloat16)
+
+    def unpack(source, side):
+        base = side * half
+        below = source[base : base + quarter].reshape(middle, middle).astype(jnp.float32)
+        mixed = source[base + quarter : base + half].reshape(middle, middle).astype(jnp.float32)
+        diagonal = source[last].astype(jnp.float32)[side : side + 1, :]
+        turned = mixed.T
+        upper_left = jnp.where(down >= across, mixed, turned)
+        lower_right = jnp.where(
+            down < across, mixed, jnp.where(down > across, turned, diagonal)
+        )
         return jnp.concatenate(
             [
-                jnp.concatenate([source[base + i * col_tiles + j] for j in range(col_tiles)], axis=1)
-                for i in range(row_tiles)
+                jnp.concatenate([upper_left, below.T], axis=1),
+                jnp.concatenate([below, lower_right], axis=1),
             ],
             axis=0,
         )
 
-    half = row_tiles * col_tiles
-    tiles_of(left_roots[1], roots_a, 0)
-    tiles_of(right_roots[1], roots_a, half)
+    carries = (lax.rem(me, 2) == 0) | (me == 1)
+    mine = jnp.where(me == 1, last, me // 2)
+
+    for load in loads:
+        load.wait()
+    pack_pair(left_roots[1], right_roots[1], roots_a)
 
     pl.semaphore_wait(barrier, holders - 1 + shards - 1)
 
@@ -205,30 +239,51 @@
 
     lax.fori_loop(1, shards, send_shard, 0)
 
-    def send_tiles(source, target, which):
-        def one(k, carry):
-            d = peer(k)
-            copy(
-                source.at[d], target.at[me], send_tile.at[which], recv_tile.at[which], d
-            ).start()
-            return carry
-
-        lax.fori_loop(1, holders, one, 0)
-        target[pl.ds(me, 1)] = source[pl.ds(me, 1)]
+    def spread_tiles(source, target, which):
+        def one(i, carry):
+            tile = lax.rem(me // 2 + i, last + 1)
+            d = jnp.where(tile == last, 1, 2 * tile)
+
+            @pl.when(d != me)
+            def _():
+                copy(
+                    source.at[tile], target.at[me], send_tile.at[which], recv_tile.at[which], d
+                ).start()
+
+            return carry
+
+        lax.fori_loop(0, last + 1, one, 0)
+
+        @pl.when(carries)
+        def _():
+            target[me] = source[mine]
 
     def pass_tiles(source, staged, target, which, row):
-        def one(k, carry):
-            d = peer(k)
-            staged[d] = source[table[row, d]]
-            copy(
-                staged.at[d], target.at[me], send_tile.at[which], recv_tile.at[which], d
-            ).start()
-            return carry
-
-        lax.fori_loop(1, holders, one, 0)
-        target[me] = source[table[row, me]]
-
-    send_tiles(roots_a, roots_b, 0)
+        @pl.when(carries)
+        def _():
+            wait_bytes(source, holders - 1, recv_tile.at[which - 1])
+
+            def one(k, carry):
+                d = peer(k)
+                staged[d] = source[table[row, d]]
+                copy(
+                    staged.at[d], target.at[mine], send_tile.at[which], recv_tile.at[which], d
+                ).start()
+                return carry
+
+            lax.fori_loop(1, holders, one, 0)
+            target[mine] = source[table[row, me]]
+
+    def wait_tiles(tiles, semaphore):
+        @pl.when(carries)
+        def _():
+            wait_bytes(tiles, last, semaphore)
+
+        @pl.when(jnp.logical_not(carries))
+        def _():
+            wait_bytes(tiles, last + 1, semaphore)
+
+    spread_tiles(roots_a, roots_b, 0)
 
     def send_gradients(c):
         def one(k, carry):
@@ -255,7 +310,6 @@
 
     lax.fori_loop(1, holders, send_sums, 0)
 
-    wait_bytes(roots_b, holders - 1, recv_tile.at[0])
     pass_tiles(roots_b, roots_c, roots_d, 1, 2)
 
     for c in range(1, CHUNKS):
@@ -269,7 +323,6 @@
         return jnp.sum(jnp.where(lane == s, clip_row, 0.0), axis=1, keepdims=True)
 
     has_first = table[4, me]
-    has_second = table[5, me]
 
     def gather_steps(c):
         wait_bytes(land.at[c], holders - 1, recv_go.at[c])
@@ -320,14 +373,16 @@
         back[c][me] = back_stage[c, me]
 
     gather_steps(0)
-    wait_bytes(roots_d, holders - 1, recv_tile.at[1])
-    root_use[0] = jnp.where(has_first > 0, left_roots[0], matrix_of(roots_d, 0))
-    root_use[1] = jnp.where(has_first > 0, right_roots[0], matrix_of(roots_d, half))
+    wait_tiles(roots_d, recv_tile.at[1])
+    for side, own in enumerate((left_roots, right_roots)):
+        sent = unpack(roots_d, side).astype(jnp.bfloat16)
+        root_use[side] = jnp.where(has_first > 0, own[0], sent)
     for c in range(CHUNKS - 1):
         directions(c)
         gather_steps(c + 1)
 
-    gram_sum[...] = jnp.zeros_like(gram_sum)
+    left_delta[0] = jnp.zeros((width, width), jnp.float32)
+    right_delta[0] = jnp.zeros((width, width), jnp.float32)
 
     def add_gram(s, carry):
         gradient = grads[s]
@@ -339,21 +394,14 @@
         right = lax.dot_general(
             gradient, gradient, (((0,), (0,)), ((), ())), preferred_element_type=jnp.float32
         )
-        gram_sum[0] = SECOND_MOMENT * gram_sum[0] + weight * left
-        gram_sum[1] = SECOND_MOMENT * gram_sum[1] + weight * right
+        left_delta[0] = SECOND_MOMENT * left_delta[0] + weight * left
+        right_delta[0] = SECOND_MOMENT * right_delta[0] + weight * right
         return carry
 
     lax.fori_loop(0, steps, add_gram, 0)
-    tiles_of(gram_sum[0].astype(jnp.bfloat16), grams_a, 0)
-    tiles_of(gram_sum[1].astype(jnp.bfloat16), grams_a, half)
-    send_tiles(grams_a, grams_b, 2)
+    pack_pair(left_delta[0], right_delta[0], grams_a)
+    spread_tiles(grams_a, grams_b, 2)
     directions(CHUNKS - 1)
-
-    kept = SECOND_MOMENT**steps
-    left_out[0] = jnp.where(has_first > 0, kept * left_stats[0] + gram_sum[0], left_stats[0])
-    right_out[0] = jnp.where(has_first > 0, kept * right_stats[0] + gram_sum[1], right_stats[0])
-
-    wait_bytes(grams_b, holders - 1, recv_tile.at[2])
     pass_tiles(grams_b, grams_c, grams_d, 3, 3)
 
     def finish(c):
@@ -372,16 +420,19 @@
     for c in range(CHUNKS):
         finish(c)
 
-    wait_bytes(grams_d, holders - 1, recv_tile.at[3])
-    left_new = kept * left_stats[1] + matrix_of(grams_d, 0).astype(jnp.float32)
-    right_new = kept * right_stats[1] + matrix_of(grams_d, half).astype(jnp.float32)
-    left_out[1] = jnp.where(has_second > 0, left_new, left_stats[1])
-    right_out[1] = jnp.where(has_second > 0, right_new, right_stats[1])
+    wait_tiles(grams_d, recv_tile.at[3])
+    left_delta[1] = unpack(grams_d, 0)
+    right_delta[1] = unpack(grams_d, 1)
 
     wait_bytes(sums_y, shards - 1, send_y)
     wait_bytes(sums_dp, holders - 1, send_dp)
-    for which in range(4):
-        wait_bytes(roots_a, holders - 1, send_tile.at[which])
+    for which in (0, 2):
+        wait_tiles(roots_a, send_tile.at[which])
+
+        @pl.when(carries)
+        def _():
+            wait_bytes(roots_b, holders - 1, send_tile.at[which + 1])
+
     for c in range(CHUNKS):
         wait_bytes(stage.at[c], holders - 1, send_go.at[c])
         wait_bytes(back_stage.at[c], holders - 1, send_back.at[c])
@@ -398,11 +449,14 @@
     message = pltpu.VMEM((CHUNKS, blocks, rows, width), bf16)
     arrivals = pltpu.VMEM((blocks, rows, width), bf16)
     by_step = pltpu.VMEM((steps, width, width), bf16)
-    tiles = pltpu.VMEM((holders, TILE_ROWS, TILE_COLS), bf16)
+    pieces = 2 * width // TILE_ROWS + 1
+    tiles = pltpu.VMEM((pieces, TILE_ROWS, TILE_COLS), bf16)
+    gathered = pltpu.VMEM((holders, TILE_ROWS, TILE_COLS), bf16)
+    roots = pltpu.VMEM(left_roots.shape, bf16)
     dma = pltpu.SemaphoreType.DMA
     vmem = pl.BlockSpec(memory_space=pltpu.VMEM)
     sizes = (steps, holders, shards, piece, width, total_count)
-    y, left, right = pl.pallas_call(
+    y, left_delta, right_delta = pl.pallas_call(
         functools.partial(kernel, sizes),
         name="shampoo",
         out_shape=(
@@ -410,9 +464,11 @@
             jax.ShapeDtypeStruct(left_stats.shape, f32),
             jax.ShapeDtypeStruct(right_stats.shape, f32),
         ),
-        in_specs=[pl.BlockSpec(memory_space=pltpu.SMEM)] + [vmem] * 5,
+        in_specs=[pl.BlockSpec(memory_space=pltpu.SMEM), vmem] + [pl.BlockSpec(memory_space=pl.ANY)] * 2,
         out_specs=(vmem,) * 3,
         scratch_shapes=[
+            roots,
+            roots,
             message,
             message,
             message,
@@ -422,15 +478,14 @@
             arrivals,
             arrivals,
             tiles,
+            gathered,
+            gathered,
             tiles,
             tiles,
-            tiles,
-            tiles,
-            tiles,
-            tiles,
+            gathered,
+            gathered,
             tiles,
             pltpu.VMEM((2, width, width), bf16),
-            pltpu.VMEM((2, width, width), f32),
             pltpu.VMEM((shards, 1, TILE_COLS), f32),
             pltpu.VMEM((holders, 1, TILE_COLS), f32),
             dma,
@@ -443,6 +498,7 @@
             dma((CHUNKS,)),
             dma((CHUNKS,)),
             dma((CHUNKS,)),
+            dma((2,)),
         ],
         compiler_params=pltpu.CompilerParams(
             collective_id=0, has_side_effects=True, vmem_limit_bytes=40 << 20
@@ -450,11 +506,13 @@
     )(
         table,
         gradients.reshape(steps, blocks * piece, width),
-        left_stats,
-        right_stats,
         left_roots,
         right_roots,
     )
+    live = table[4:6, lax.axis_index("dp")][:, None, None] > 0
+    kept = SECOND_MOMENT**steps
+    left = jnp.where(live, kept * left_stats + left_delta, left_stats)
+    right = jnp.where(live, kept * right_stats + right_delta, right_stats)
     return y.reshape(gradients.shape), left, right
 
 

time: 97.7 us -> 86.6 us (0.89)
  Pallas kernels: 87.2 us -> 77.4 us
  local copies, waits for them, and re-layouts: 7.86 us -> 4.1 us
  other arithmetic: 1.6 us -> 4.16 us
    pallas_call x1, Pallas kernels: 87.2 us -> 77.4 us  [shards_step(): pl.pallas_call(functools.partial(kernel, sizes), name='shampoo', out_shap...]
    unnamed x20 -> x6, local copies, waits for them, and re-layouts: 5.31 us -> 1.6 us
    select_n x0 -> x1, other arithmetic: none -> 2.37 us  [shards_step(): right = jnp.where(live, kept * right_stats + right_delta, right_stats)]
where the time goes in v2:
time: 86.6 us; the launch traced here: 86.4 us
  Pallas kernels  77.4 us (89%)
  other arithmetic  4.16 us (5%)
  local copies, waits for them, and re-layouts  4.1 us (5%)
    pallas_call x1, Pallas kernels, shards_step(): pl.pallas_call(functools.partial(kernel, sizes), name='shampoo', out_shap...  77.4 us
    select_n x1, other arithmetic, shards_step(): right = jnp.where(live, kept * right_stats + right_delta, right_stats)  2.37 us

profile of v2, /device:TPU:1, one launch (start us, length us, event | category | flops | bytes accessed | tf_op | source)
XLA Modules:
  0.0 86.4 jit_solution(8672627027893033861)
XLA Ops:
  0.6 0.9 %convert_reduce_fusion.2 = s32[64]{0:T(128)S(1)} fusion(s32[64]{0:T(128)} %param.7), kind=kLoop, calls=%fused_computation.11 | loop fusion | flops 20416 | bytes 512 | tf_op jit(solution)/shard_map/reduce_sum | solution.py:24
  1.6 0.0 copy-start.2
  1.6 0.6 copy-done.2
  2.2 0.1 fusion.6
  2.3 0.2 select_reduce_fusion.4
  2.5 0.1 convert_reduce_fusion.1
  2.6 0.2 select_reduce_fusion
  2.8 0.1 select_reduce_fusion.2
  2.9 0.0 copy-start
  3.0 1.4 %reshape.82.x_ref = bf16[8,256,256]{2,1,0:T(8,128)(2,1)S(1)} reshape(bf16[8,64,4,256]{3,2,1,0:T(4,128)(2,1)} %param.6) | data formatting | bytes 2097152 | tf_op jit(solution)/shard_map/reshape | solution.py:508
  4.4 0.0 copy-done
  4.4 0.0 copy-start.1
  4.4 0.9 %copy-done.1 = bf16[2,256,256]{2,1,0:T(8,128)(2,1)S(1)} copy-done((bf16[2,256,256]{2,1,0:T(8,128)(2,1)S(1)}, bf16[2,256,256]{2,1,0:T(8,128)(2,1)}, u32[]{:S(2)}) %copy-start.1) | copy-done | bytes 262168
  5.3 77.4 %shampoo.1 = (bf16[8,256,256]{2,1,0:T(8,128)(2,1)S(1)}, f32[2,256,256]{2,1,0:T(8,128)S(1)}, f32[2,256,256]{2,1,0:T(8,128)S(1)}) custom-call(s32[6,64]{1,0:T(8,128)S(1)} %stack.18.table, bf16[8,256,256]{2,1,0:T(8,128)(2,1)S(1)} %reshape.82.x_ref, bf16[2,256,256]{2,1,0:T(8,128)(2,1)S(1)} %copy-done, bf16[2,256,256]{2,1,0:T(8,128)(2,1)S(1)} %copy-done.1), custom_call_target="tpu_custom_call" | custom-call | tf_op jit(solution)/shard_map/shampoo/pallas_call | solution.py:459
  82.7 0.2 compare_reduce_fusion
  82.9 2.4 %add_select_fusion = (f32[2,256,256]{2,1,0:T(8,128)}, f32[2,256,256]{2,1,0:T(8,128)}) fusion(f32[2,256,256]{2,1,0:T(8,128)} %param.9, f32[2,256,256]{2,1,0:T(8,128)S(1)} %get-tuple-element.8, pred[2]{0:T(512)(128)(4,1)S(1)} %compare_reduce_fusion, f32[2,256,256]{2,1,0:T(8,128)} %param.8, f32[2,256,256]{2,1,0:T(8,128)S(1)} %get-tuple-element.7), kind=kLoop, calls=%fused_computation | loop fusion | flops 786432 | bytes 3145730 | tf_op jit(solution)/shard_map/jit(_where)/select_n | solution.py:515
  85.3 1.1 %reshape.83 = bf16[8,64,4,256]{3,2,1,0:T(4,128)(2,1)} reshape(bf16[8,256,256]{2,1,0:T(8,128)(2,1)S(1)} %get-tuple-element.6) | data formatting | bytes 2097152 | tf_op jit(solution)/shard_map/reshape | solution.py:516
  (5 shorter events, 0.0 us)
Async XLA Ops:
  1.6 0.7 copy-start.2
  2.9 1.4 %copy-start = (bf16[2,256,256]{2,1,0:T(8,128)(2,1)S(1)}, bf16[2,256,256]{2,1,0:T(8,128)(2,1)}, u32[]{:S(2)}) copy-start(bf16[2,256,256]{2,1,0:T(8,128)(2,1)} %left_hbm.1) | copy-start | bytes 786436
  4.4 1.0 %copy-start.1 = (bf16[2,256,256]{2,1,0:T(8,128)(2,1)S(1)}, bf16[2,256,256]{2,1,0:T(8,128)(2,1)}, u32[]{:S(2)}) copy-start(bf16[2,256,256]{2,1,0:T(8,128)(2,1)} %right_hbm.1) | copy-start | bytes 786436

commit v3 on v2

--- a/solution.py
+++ b/solution.py
@@ -13,58 +13,62 @@
 MESH = pl.DeviceIdType.MESH
 
 CHUNKS = 2
+VMEM_BYTES = 56 << 20
 TILE_ROWS, TILE_COLS = 16, 128
 
 
-def routes(owners):
-    count = owners.shape[0]
-    position = jnp.arange(count, dtype=jnp.int32)
-    same_owner = owners[:, None] == owners[None, :]
-    earlier = position[None, :] < position[:, None]
-    slot = jnp.sum((same_owner & earlier).astype(jnp.int32), axis=1)
-    owned = owners[None, :] == position[:, None]
-    first = owned & (slot == 0)[None, :]
-    second = owned & (slot == 1)[None, :]
-    has_first = jnp.any(first, axis=1)
-    has_second = jnp.any(second, axis=1)
-    first_block = jnp.sum(jnp.where(first, position[None, :], 0), axis=1)
-    second_block = jnp.sum(jnp.where(second, position[None, :], 0), axis=1)
-    before = position[None, :] < position[:, None]
-    empty_rank = jnp.sum((before & ~has_first[None, :]).astype(jnp.int32), axis=1)
-    second_rank = jnp.sum((before & has_second[None, :]).astype(jnp.int32), axis=1)
-    match = (
-        (empty_rank[:, None] == second_rank[None, :])
-        & ~has_first[:, None]
-        & has_second[None, :]
-    )
-    helped = jnp.sum(jnp.where(match, position[None, :], 0), axis=1)
-    helper = jnp.sum(jnp.where(match, position[:, None], 0), axis=0)
-    helped_block = jnp.sum(jnp.where(match, second_block[None, :], 0), axis=1)
-    block_of = jnp.where(has_first, first_block, helped_block)
-    device_of = jnp.sum(
-        jnp.where(block_of[:, None] == position[None, :], position[:, None], 0), axis=0
-    )
-    return jnp.stack(
-        [
-            block_of,
-            device_of,
-            helped,
-            helper,
-            has_first.astype(jnp.int32),
-            has_second.astype(jnp.int32),
-        ]
-    )
+def routes(owner_row):
+    count = owner_row.shape[1]
+    down = lax.broadcasted_iota(jnp.int32, (count, count), 0)
+    across = lax.broadcasted_iota(jnp.int32, (count, count), 1)
+
+    def along(mask, value, axis):
+        return jnp.sum(jnp.where(mask, value, 0), axis=axis, keepdims=True)
+
+    def column(row):
+        return along(down == across, row, 1)
+
+    def row(col):
+        return along(down == across, col, 0)
+
+    slot = along((column(owner_row) == owner_row) & (down < across), 1, 0)
+    owned = owner_row == down
+    load = along(owned, 1, 1)
+    load_row = row(load)
+    first_block = along(owned & (slot == 0), across, 1)
+    second_block = along(owned & (slot == 1), across, 1)
+    empty_rank = along((across < down) & (load_row == 0), 1, 1)
+    second_rank = along((down < across) & (load > 1), 1, 0)
+    match = (empty_rank == second_rank) & (load == 0) & (load_row > 1)
+    helped = along(match, across, 1)
+    helper = along(match, down, 0)
+    helped_block = along(match, row(second_block), 1)
+    block_of = jnp.where(load > 0, first_block, helped_block)
+    device_of = along(block_of == across, down, 0)
+    tables = (row(block_of), device_of, row(helped), helper)
+    return tuple(jnp.minimum(table, count - 1) for table in tables) + (load_row,)
 
 
 def kernel(
     sizes,
+    owners_hbm,
+    x_hbm,
+    left_hbm,
+    right_hbm,
+    left_old_hbm,
+    right_old_hbm,
+    y_hbm,
+    left_new_hbm,
+    right_new_hbm,
+    y_ref,
+    left_new,
+    right_new,
+    left_old,
+    right_old,
+    owners_ref,
+    table_ref,
     table,
     x_ref,
-    left_hbm,
-    right_hbm,
-    y_ref,
-    left_delta,
-    right_delta,
     left_roots,
     right_roots,
     byblock,
@@ -97,6 +101,7 @@
     send_back,
     recv_back,
     load_sem,
+    store_sem,
 ):
     steps, holders, shards, piece, width, total_count = sizes
     back = (back_first, back_second)
@@ -126,22 +131,21 @@
     lax.fori_loop(1, shards, greet_shard, 0)
     lax.fori_loop(1, holders, greet, 0)
 
-    loads = (
-        pltpu.make_async_copy(left_hbm, left_roots, load_sem.at[0]),
-        pltpu.make_async_copy(right_hbm, right_roots, load_sem.at[1]),
-    )
+    loads = [
+        pltpu.make_async_copy(source, target, load_sem.at[i])
+        for i, (source, target) in enumerate(
+            (
+                (left_hbm, left_roots),
+                (right_hbm, right_roots),
+                (owners_hbm, owners_ref),
+                (x_hbm, x_ref),
+                (left_old_hbm, left_old),
+                (right_old_hbm, right_old),
+            )
+        )
+    ]
     for load in loads:
         load.start()
-
-    lane = lax.broadcasted_iota(jnp.int32, (1, TILE_COLS), 1)
-
-    def add_square(s, row):
-        values = x_ref[s].astype(jnp.float32)
-        square = jnp.sum(values * values, axis=(0, 1), keepdims=True)
-        return row + jnp.where(lane == s, square, 0.0)
-
-    local_row = lax.fori_loop(0, steps, add_square, jnp.zeros((1, TILE_COLS), jnp.float32))
-    sums_y[pl.ds(shard, 1)] = local_row[None]
 
     out_index = lax.broadcasted_iota(jnp.int32, (width, width), 0)
     in_index = lax.broadcasted_iota(jnp.int32, (width, width), 1)
@@ -156,16 +160,10 @@
     def permute(matrix, values):
         return jnp.dot(matrix, values, preferred_element_type=jnp.float32).astype(jnp.bfloat16)
 
-    def split_by_device(c, g, source, target):
-        part = source[pl.ds(c * chunk_steps, chunk_steps), pl.ds(g * span, span), :]
-        done = permute(apart, part.reshape(width, width))
-        target[c, pl.ds(g * group, group)] = done.reshape(group, rows, width)
-
-    def prepare(i, carry):
-        split_by_device(i // groups, i % groups, x_ref, byblock)
-        return carry
-
-    lax.fori_loop(0, CHUNKS * groups, prepare, 0)
+    def split_by_device(part):
+        return jnp.dot(
+            apart, part.reshape(width, width), preferred_element_type=jnp.float32
+        ).reshape(group, rows, width)
 
     middle = width // 2
     quarter = middle // TILE_ROWS
@@ -212,9 +210,33 @@
     carries = (lax.rem(me, 2) == 0) | (me == 1)
     mine = jnp.where(me == 1, last, me // 2)
 
-    for load in loads:
-        load.wait()
+    loads[0].wait()
+    loads[1].wait()
     pack_pair(left_roots[1], right_roots[1], roots_a)
+    loads[2].wait()
+    table_ref[...] = jnp.zeros_like(table_ref)
+    for i, values in enumerate(routes(owners_ref[...])):
+        table_ref[i : i + 1, :holders] = values
+    table_copy = pltpu.make_async_copy(table_ref, table, load_sem.at[6])
+    table_copy.start()
+    loads[3].wait()
+
+    lane = lax.broadcasted_iota(jnp.int32, (rows, TILE_COLS), 1)
+    step_of = lax.broadcasted_iota(jnp.int32, (rows, TILE_COLS), 0) // piece
+    local_row = jnp.zeros((1, TILE_COLS), jnp.float32)
+    for c in range(CHUNKS):
+
+        def prepare(g, total, c=c):
+            part = x_ref[pl.ds(c * chunk_steps, chunk_steps), pl.ds(g * group, group)]
+            done = split_by_device(part)
+            byblock[c, pl.ds(g * group, group)] = done.astype(jnp.bfloat16)
+            return total + jnp.sum(done * done, axis=0)
+
+        squares = lax.fori_loop(0, groups, prepare, jnp.zeros((rows, width), jnp.float32))
+        by_row = jnp.sum(squares, axis=1, keepdims=True)
+        spot = lane == step_of + c * chunk_steps
+        local_row = local_row + jnp.sum(jnp.where(spot, by_row, 0.0), axis=0, keepdims=True)
+    sums_y[pl.ds(shard, 1)] = local_row[None]
 
     pl.semaphore_wait(barrier, holders - 1 + shards - 1)
 
@@ -285,6 +307,8 @@
 
     spread_tiles(roots_a, roots_b, 0)
 
+    table_copy.wait()
+
     def send_gradients(c):
         def one(k, carry):
             d = peer(k)
@@ -320,9 +344,9 @@
     clip_row = jnp.minimum(1.0, 1.0 / jnp.sqrt(totals / total_count + CLIP_EPSILON))
 
     def clip_of(s):
-        return jnp.sum(jnp.where(lane == s, clip_row, 0.0), axis=1, keepdims=True)
-
-    has_first = table[4, me]
+        return jnp.sum(jnp.where(lane[:1] == s, clip_row, 0.0), axis=1, keepdims=True)
+
+    load = table[4, me]
 
     def gather_steps(c):
         wait_bytes(land.at[c], holders - 1, recv_go.at[c])
@@ -357,7 +381,8 @@
         lax.fori_loop(c * chunk_steps, (c + 1) * chunk_steps, one, 0)
 
         def sort(g, carry):
-            split_by_device(c, g, outs, back_stage)
+            part = outs[pl.ds(c * chunk_steps, chunk_steps), pl.ds(g * span, span), :]
+            back_stage[c, pl.ds(g * group, group)] = split_by_device(part).astype(jnp.bfloat16)
             return carry
 
         lax.fori_loop(0, groups, sort, 0)
@@ -376,13 +401,13 @@
     wait_tiles(roots_d, recv_tile.at[1])
     for side, own in enumerate((left_roots, right_roots)):
         sent = unpack(roots_d, side).astype(jnp.bfloat16)
-        root_use[side] = jnp.where(has_first > 0, own[0], sent)
+        root_use[side] = jnp.where(load > 0, own[0], sent)
     for c in range(CHUNKS - 1):
         directions(c)
         gather_steps(c + 1)
 
-    left_delta[0] = jnp.zeros((width, width), jnp.float32)
-    right_delta[0] = jnp.zeros((width, width), jnp.float32)
+    left_new[0] = jnp.zeros((width, width), jnp.float32)
+    right_new[0] = jnp.zeros((width, width), jnp.float32)
 
     def add_gram(s, carry):
         gradient = grads[s]
@@ -394,14 +419,29 @@
         right = lax.dot_general(
             gradient, gradient, (((0,), (0,)), ((), ())), preferred_element_type=jnp.float32
         )
-        left_delta[0] = SECOND_MOMENT * left_delta[0] + weight * left
-        right_delta[0] = SECOND_MOMENT * right_delta[0] + weight * right
+        left_new[0] = SECOND_MOMENT * left_new[0] + weight * left
+        right_new[0] = SECOND_MOMENT * right_new[0] + weight * right
         return carry
 
     lax.fori_loop(0, steps, add_gram, 0)
-    pack_pair(left_delta[0], right_delta[0], grams_a)
+    pack_pair(left_new[0], right_new[0], grams_a)
     spread_tiles(grams_a, grams_b, 2)
     directions(CHUNKS - 1)
+
+    kept = SECOND_MOMENT**steps
+    stores = []
+
+    def store(source, target):
+        done = pltpu.make_async_copy(source, target, store_sem.at[len(stores)])
+        done.start()
+        stores.append(done)
+
+    sides = ((left_old, left_new, left_new_hbm), (right_old, right_new, right_new_hbm))
+    for side, (old, new, target) in enumerate(sides):
+        loads[4 + side].wait()
+        new[0] = jnp.where(load > 0, kept * old[0] + new[0], old[0])
+        store(new.at[0], target.at[0])
+
     pass_tiles(grams_b, grams_c, grams_d, 3, 3)
 
     def finish(c):
@@ -411,18 +451,21 @@
             values = jnp.concatenate(
                 [back[c][table[1, g * group + i]] for i in range(group)], axis=0
             )
-            done = permute(together, values).reshape(chunk_steps, span, width)
-            y_ref[pl.ds(c * chunk_steps, chunk_steps), pl.ds(g * span, span), :] = done
+            done = permute(together, values).reshape(chunk_steps, group, piece, width)
+            y_ref[pl.ds(c * chunk_steps, chunk_steps), pl.ds(g * group, group)] = done
             return carry
 
         lax.fori_loop(0, groups, one, 0)
+        part = pl.ds(c * chunk_steps, chunk_steps)
+        store(y_ref.at[part], y_hbm.at[part])
 
     for c in range(CHUNKS):
         finish(c)
 
     wait_tiles(grams_d, recv_tile.at[3])
-    left_delta[1] = unpack(grams_d, 0)
-    right_delta[1] = unpack(grams_d, 1)
+    for side, (old, new, target) in enumerate(sides):
+        new[1] = jnp.where(load > 1, kept * old[1] + unpack(grams_d, side), old[1])
+        store(new.at[1], target.at[1])
 
     wait_bytes(sums_y, shards - 1, send_y)
     wait_bytes(sums_dp, holders - 1, send_dp)
@@ -436,6 +479,25 @@
     for c in range(CHUNKS):
         wait_bytes(stage.at[c], holders - 1, send_go.at[c])
         wait_bytes(back_stage.at[c], holders - 1, send_back.at[c])
+    for done in stores:
+        done.wait()
+
+
+def hand_over(count, *refs):
+    inputs, outputs, rooms = refs[:count], refs[count : 2 * count], refs[2 * count : 3 * count]
+    load_sem, store_sem = refs[3 * count :]
+    parts = [(k, i) for k in range(count) for i in range(inputs[k].shape[0])]
+    loads, stores = [], []
+    for n, (k, i) in enumerate(parts):
+        loads.append(pltpu.make_async_copy(inputs[k].at[i], rooms[k].at[i], load_sem.at[n]))
+        stores.append(pltpu.make_async_copy(rooms[k].at[i], outputs[k].at[i], store_sem.at[n]))
+    for load in loads:
+        load.start()
+    for load, store in zip(loads, stores):
+        load.wait()
+        store.start()
+    for store in stores:
+        store.wait()
 
 
 def shards_step(gradients, owners, left_stats, right_stats, left_roots, right_roots):
@@ -444,7 +506,6 @@
     shards = lax.axis_size("tensor")
     rows = piece * (steps // CHUNKS)
     total_count = float(holders * shards * blocks * piece * width)
-    table = routes(owners)
     bf16, f32 = jnp.bfloat16, jnp.float32
     message = pltpu.VMEM((CHUNKS, blocks, rows, width), bf16)
     arrivals = pltpu.VMEM((blocks, rows, width), bf16)
@@ -454,19 +515,30 @@
     gathered = pltpu.VMEM((holders, TILE_ROWS, TILE_COLS), bf16)
     roots = pltpu.VMEM(left_roots.shape, bf16)
     dma = pltpu.SemaphoreType.DMA
-    vmem = pl.BlockSpec(memory_space=pltpu.VMEM)
+    hbm = pl.BlockSpec(memory_space=pl.ANY)
     sizes = (steps, holders, shards, piece, width, total_count)
-    y, left_delta, right_delta = pl.pallas_call(
+    outs = (
+        jax.ShapeDtypeStruct(gradients.shape, bf16),
+        jax.ShapeDtypeStruct(left_stats.shape, f32),
+        jax.ShapeDtypeStruct(right_stats.shape, f32),
+    )
+    stats = pltpu.VMEM(left_stats.shape, f32)
+    results = pl.pallas_call(
         functools.partial(kernel, sizes),
         name="shampoo",
-        out_shape=(
-            jax.ShapeDtypeStruct((steps, blocks * piece, width), bf16),
-            jax.ShapeDtypeStruct(left_stats.shape, f32),
-            jax.ShapeDtypeStruct(right_stats.shape, f32),
-        ),
-        in_specs=[pl.BlockSpec(memory_space=pltpu.SMEM), vmem] + [pl.BlockSpec(memory_space=pl.ANY)] * 2,
-        out_specs=(vmem,) * 3,
+        out_shape=outs,
+        in_specs=[hbm] * 6,
+        out_specs=(hbm,) * 3,
         scratch_shapes=[
+            pltpu.VMEM(gradients.shape, bf16),
+            stats,
+            stats,
+            stats,
+            stats,
+            pltpu.VMEM((1, blocks), jnp.int32),
+            pltpu.VMEM((8, TILE_COLS), jnp.int32),
+            pltpu.SMEM((8, TILE_COLS), jnp.int32),
+            pltpu.VMEM(gradients.shape, bf16),
             roots,
             roots,
             message,
@@ -498,22 +570,24 @@
             dma((CHUNKS,)),
             dma((CHUNKS,)),
             dma((CHUNKS,)),
-            dma((2,)),
+            dma((7,)),
+            dma((CHUNKS + 4,)),
         ],
         compiler_params=pltpu.CompilerParams(
-            collective_id=0, has_side_effects=True, vmem_limit_bytes=40 << 20
+            collective_id=0, has_side_effects=True, vmem_limit_bytes=VMEM_BYTES
         ),
-    )(
-        table,
-        gradients.reshape(steps, blocks * piece, width),
-        left_roots,
-        right_roots,
-    )
-    live = table[4:6, lax.axis_index("dp")][:, None, None] > 0
-    kept = SECOND_MOMENT**steps
-    left = jnp.where(live, kept * left_stats + left_delta, left_stats)
-    right = jnp.where(live, kept * right_stats + right_delta, right_stats)
-    return y.reshape(gradients.shape), left, right
+    )(owners.reshape(1, blocks), gradients, left_roots, right_roots, left_stats, right_stats)
+    parts = sum(out.shape[0] for out in outs)
+    return pl.pallas_call(
+        functools.partial(hand_over, len(outs)),
+        name="hand_over",
+        out_shape=outs,
+        in_specs=[hbm] * 3,
+        out_specs=(hbm,) * 3,
+        scratch_shapes=[pltpu.VMEM(out.shape, out.dtype) for out in outs]
+        + [dma((parts,)), dma((parts,))],
+        compiler_params=pltpu.CompilerParams(vmem_limit_bytes=VMEM_BYTES),
+    )(*results)
 
 
 def solution(mesh):

time: 86.6 us -> 81.2 us (0.938)
  other arithmetic: 4.16 us -> 0 us
  local copies, waits for them, and re-layouts: 4.1 us -> 0 us
  Pallas kernels: 77.4 us -> 80.4 us
    pallas_call x0 -> x1, Pallas kernels: none -> 2.54 us  [shards_step(): pl.pallas_call(functools.partial(hand_over, len(outs)), name='hand_over',...]
    reshape x2 -> x0, local copies, waits for them, and re-layouts: 2.48 us -> none  [the longest x1 1.38 us: shards_step(): gradients.reshape(steps, blocks * piece, width)]
    select_n x2 -> x0, other arithmetic: 2.38 us -> none  [the longest x1 2.37 us: shards_step(): right = jnp.where(live, kept * right_stats + right_delta, right_stats)]
    unnamed x6 -> x0, local copies, waits for them, and re-layouts: 1.6 us -> none
    reduce_sum x5 -> x0, other arithmetic: 1.47 us -> none  [the longest x1 0.91 us: routes(): slot = jnp.sum((same_owner & earlier).astype(jnp.int32), axis=1)]
where the time goes in v3:
time: 81.2 us; the launch traced here: 81 us
  Pallas kernels  80.4 us (99%)
    pallas_call x1, Pallas kernels, shards_step(): pl.pallas_call(functools.partial(kernel, sizes), name='shampoo', out_shap...  77.8 us
    pallas_call x1, Pallas kernels, shards_step(): pl.pallas_call(functools.partial(hand_over, len(outs)), name='hand_over',...  2.54 us

profile of v3, /device:TPU:1, one launch (start us, length us, event | category | flops | bytes accessed | tf_op | source)
XLA Modules:
  0.0 81.0 jit_solution(7184369138574131072)
XLA Ops:
  0.6 77.8 %shampoo.1 = (bf16[8,64,4,256]{3,2,1,0:T(4,128)(2,1)}, f32[2,256,256]{2,1,0:T(8,128)}, f32[2,256,256]{2,1,0:T(8,128)}) custom-call(s32[1,64]{1,0:T(1,128)} %bitcast.1, bf16[8,64,4,256]{3,2,1,0:T(4,128)(2,1)} %x_hbm.1, bf16[2,256,256]{2,1,0:T(8,128)(2,1)} %left_hbm.1, bf16[2,256,256]{2,1,0:T(8,128)(2,1)} %right_hbm.1, f32[2,256,256]{2,1,0:T(8,128)} %left_old_hbm.1, ...), custom_call_target="tpu_custom_call" | custom-call | tf_op jit(solution)/shard_map/shampoo/pallas_call | solution.py:526
  78.5 2.5 %hand_over.1 = (bf16[8,64,4,256]{3,2,1,0:T(4,128)(2,1)}, f32[2,256,256]{2,1,0:T(8,128)}, f32[2,256,256]{2,1,0:T(8,128)}) custom-call(bf16[8,64,4,256]{3,2,1,0:T(4,128)(2,1)} %get-tuple-element.6.refs_0_, f32[2,256,256]{2,1,0:T(8,128)} %get-tuple-element.7.refs_1_, f32[2,256,256]{2,1,0:T(8,128)} %get-tuple-element.8.refs_2_), custom_call_target="tpu_custom_call" | custom-call | tf_op jit(solution)/shard_map/hand_over/pallas_call | solution.py:581

commit v4 on v3

--- a/solution.py
+++ b/solution.py
@@ -87,6 +87,11 @@
     grams_b,
     grams_c,
     grams_d,
+    diag_a,
+    diag_b_roots,
+    diag_b_grams,
+    diag_c,
+    diag_d,
     root_use,
     sums_y,
     sums_dp,
@@ -96,6 +101,8 @@
     recv_dp,
     send_tile,
     recv_tile,
+    send_diag,
+    recv_diag,
     send_go,
     recv_go,
     send_back,
@@ -113,8 +120,14 @@
     me = lax.axis_index("dp")
     shard = lax.axis_index("tensor")
 
+    plane = holders // 8
+
     def peer(k):
-        return lax.rem(me + k, holders)
+        i = k - 1
+        far = i < 7 * plane
+        up = jnp.where(far, i % 7 + 1, 0)
+        along = jnp.where(far, i // 7, i - 7 * plane + 1)
+        return (me // plane + up) % 8 * plane + (me + along) % plane
 
     barrier = pltpu.get_barrier_semaphore()
 
@@ -168,7 +181,8 @@
     middle = width // 2
     quarter = middle // TILE_ROWS
     half = 2 * quarter
-    last = 2 * half
+    count = 2 * half
+    diag_b = (diag_b_roots, diag_b_grams)
     down = lax.broadcasted_iota(jnp.int32, (middle, middle), 0)
     across = lax.broadcasted_iota(jnp.int32, (middle, middle), 1)
 
@@ -181,19 +195,15 @@
         target[base + quarter : base + half] = mixed.reshape(quarter, TILE_ROWS, middle)
         return jnp.sum(jnp.where(down == across, lower_right, 0.0), axis=0, keepdims=True)
 
-    def pack_pair(left, right, target):
-        left_diagonal = pack(left, target, 0)
-        right_diagonal = pack(right, target, half)
-        row = lax.broadcasted_iota(jnp.int32, (TILE_ROWS, middle), 0)
-        target[last] = jnp.where(
-            row == 0, left_diagonal, jnp.where(row == 1, right_diagonal, 0.0)
-        ).astype(jnp.bfloat16)
-
-    def unpack(source, side):
+    def pack_pair(left, right, target, kind):
+        diag_a[kind, 0] = pack(left, target, 0)
+        diag_a[kind, 1] = pack(right, target, half)
+
+    def unpack(source, side, kind):
         base = side * half
         below = source[base : base + quarter].reshape(middle, middle).astype(jnp.float32)
         mixed = source[base + quarter : base + half].reshape(middle, middle).astype(jnp.float32)
-        diagonal = source[last].astype(jnp.float32)[side : side + 1, :]
+        diagonal = diag_d[kind, side]
         turned = mixed.T
         upper_left = jnp.where(down >= across, mixed, turned)
         lower_right = jnp.where(
@@ -207,12 +217,15 @@
             axis=0,
         )
 
-    carries = (lax.rem(me, 2) == 0) | (me == 1)
-    mine = jnp.where(me == 1, last, me // 2)
+    carries = lax.rem(me, 2) == 0
+    mine = me // 2
+    homes = (1, holders // 2 + 1)
+    holds = (me == homes[0]) | (me == homes[1])
+    my_side = jnp.where(me == homes[1], 1, 0)
 
     loads[0].wait()
     loads[1].wait()
-    pack_pair(left_roots[1], right_roots[1], roots_a)
+    pack_pair(left_roots[1], right_roots[1], roots_a, 0)
     loads[2].wait()
     table_ref[...] = jnp.zeros_like(table_ref)
     for i, values in enumerate(routes(owners_ref[...])):
@@ -263,8 +276,12 @@
 
     def spread_tiles(source, target, which):
         def one(i, carry):
-            tile = lax.rem(me // 2 + i, last + 1)
-            d = jnp.where(tile == last, 1, 2 * tile)
+            chips = plane // 2
+            far = i < 7 * chips
+            up = jnp.where(far, i % 7 + 1, 0)
+            along = jnp.where(far, i // 7, i - 7 * chips)
+            chip = (me // plane + up) % 8 * chips + (me // 2 + along) % chips
+            tile, d = chip, 2 * chip
 
             @pl.when(d != me)
             def _():
@@ -274,11 +291,28 @@
 
             return carry
 
-        lax.fori_loop(0, last + 1, one, 0)
+        lax.fori_loop(0, count, one, 0)
 
         @pl.when(carries)
         def _():
             target[me] = source[mine]
+
+        kind = which // 2
+        for side, d in enumerate(homes):
+
+            @pl.when(me != d)
+            def _(side=side, d=d):
+                copy(
+                    diag_a.at[kind, side],
+                    diag_b[kind].at[me],
+                    send_diag.at[which],
+                    recv_diag.at[which],
+                    d,
+                ).start()
+
+            @pl.when(me == d)
+            def _(side=side):
+                diag_b[kind][me] = diag_a[kind, side]
 
     def pass_tiles(source, staged, target, which, row):
         @pl.when(carries)
@@ -296,14 +330,43 @@
             lax.fori_loop(1, holders, one, 0)
             target[mine] = source[table[row, me]]
 
-    def wait_tiles(tiles, semaphore):
+        @pl.when(holds)
+        def _():
+            kind = which // 2
+            rows_in = diag_b[kind]
+            wait_bytes(rows_in, holders - 1, recv_diag.at[which - 1])
+
+            def one(k, carry):
+                d = peer(k)
+                diag_c[kind, d] = rows_in[table[row, d]]
+                copy(
+                    diag_c.at[kind, d],
+                    diag_d.at[kind, my_side],
+                    send_diag.at[which],
+                    recv_diag.at[which],
+                    d,
+                ).start()
+                return carry
+
+            lax.fori_loop(1, holders, one, 0)
+            diag_d[kind, my_side] = rows_in[table[row, me]]
+
+    def wait_tiles(tiles, semaphore, diagonal_semaphore):
         @pl.when(carries)
         def _():
-            wait_bytes(tiles, last, semaphore)
+            wait_bytes(tiles, count - 1, semaphore)
 
         @pl.when(jnp.logical_not(carries))
         def _():
-            wait_bytes(tiles, last + 1, semaphore)
+            wait_bytes(tiles, count, semaphore)
+
+        @pl.when(holds)
+        def _():
+            wait_bytes(diag_d.at[0], 1, diagonal_semaphore)
+
+        @pl.when(jnp.logical_not(holds))
+        def _():
+            wait_bytes(diag_d.at[0], 2, diagonal_semaphore)
 
     spread_tiles(roots_a, roots_b, 0)
 
@@ -397,15 +460,6 @@
         lax.fori_loop(1, holders, send, 0)
         back[c][me] = back_stage[c, me]
 
-    gather_steps(0)
-    wait_tiles(roots_d, recv_tile.at[1])
-    for side, own in enumerate((left_roots, right_roots)):
-        sent = unpack(roots_d, side).astype(jnp.bfloat16)
-        root_use[side] = jnp.where(load > 0, own[0], sent)
-    for c in range(CHUNKS - 1):
-        directions(c)
-        gather_steps(c + 1)
-
     left_new[0] = jnp.zeros((width, width), jnp.float32)
     right_new[0] = jnp.zeros((width, width), jnp.float32)
 
@@ -423,8 +477,21 @@
         right_new[0] = SECOND_MOMENT * right_new[0] + weight * right
         return carry
 
-    lax.fori_loop(0, steps, add_gram, 0)
-    pack_pair(left_new[0], right_new[0], grams_a)
+    def add_grams(c):
+        lax.fori_loop(c * chunk_steps, (c + 1) * chunk_steps, add_gram, 0)
+
+    gather_steps(0)
+    wait_tiles(roots_d, recv_tile.at[1], recv_diag.at[1])
+    for side, own in enumerate((left_roots, right_roots)):
+        sent = unpack(roots_d, side, 0).astype(jnp.bfloat16)
+        root_use[side] = jnp.where(load > 0, own[0], sent)
+    for c in range(CHUNKS - 1):
+        directions(c)
+        add_grams(c)
+        gather_steps(c + 1)
+    add_grams(CHUNKS - 1)
+
+    pack_pair(left_new[0], right_new[0], grams_a, 1)
     spread_tiles(grams_a, grams_b, 2)
     directions(CHUNKS - 1)
 
@@ -462,19 +529,23 @@
     for c in range(CHUNKS):
         finish(c)
 
-    wait_tiles(grams_d, recv_tile.at[3])
+    wait_tiles(grams_d, recv_tile.at[3], recv_diag.at[3])
     for side, (old, new, target) in enumerate(sides):
-        new[1] = jnp.where(load > 1, kept * old[1] + unpack(grams_d, side), old[1])
+        new[1] = jnp.where(load > 1, kept * old[1] + unpack(grams_d, side, 1), old[1])
         store(new.at[1], target.at[1])
 
     wait_bytes(sums_y, shards - 1, send_y)
     wait_bytes(sums_dp, holders - 1, send_dp)
     for which in (0, 2):
-        wait_tiles(roots_a, send_tile.at[which])
+        wait_tiles(roots_a, send_tile.at[which], send_diag.at[which])
 
         @pl.when(carries)
         def _():
             wait_bytes(roots_b, holders - 1, send_tile.at[which + 1])
+
+        @pl.when(holds)
+        def _():
+            wait_bytes(diag_b_roots, holders - 1, send_diag.at[which + 1])
 
     for c in range(CHUNKS):
         wait_bytes(stage.at[c], holders - 1, send_go.at[c])
@@ -510,9 +581,11 @@
     message = pltpu.VMEM((CHUNKS, blocks, rows, width), bf16)
     arrivals = pltpu.VMEM((blocks, rows, width), bf16)
     by_step = pltpu.VMEM((steps, width, width), bf16)
-    pieces = 2 * width // TILE_ROWS + 1
+    pieces = 2 * width // TILE_ROWS
     tiles = pltpu.VMEM((pieces, TILE_ROWS, TILE_COLS), bf16)
     gathered = pltpu.VMEM((holders, TILE_ROWS, TILE_COLS), bf16)
+    diagonals = pltpu.VMEM((2, 2, 1, TILE_COLS), f32)
+    one_per_device = pltpu.VMEM((holders, 1, TILE_COLS), f32)
     roots = pltpu.VMEM(left_roots.shape, bf16)
     dma = pltpu.SemaphoreType.DMA
     hbm = pl.BlockSpec(memory_space=pl.ANY)
@@ -557,6 +630,11 @@
             gathered,
             gathered,
             tiles,
+            diagonals,
+            one_per_device,
+            one_per_device,
+            pltpu.VMEM((2, holders, 1, TILE_COLS), f32),
+            diagonals,
             pltpu.VMEM((2, width, width), bf16),
             pltpu.VMEM((shards, 1, TILE_COLS), f32),
             pltpu.VMEM((holders, 1, TILE_COLS), f32),
@@ -564,6 +642,8 @@
             dma,
             dma,
             dma,
+            dma((4,)),
+            dma((4,)),
             dma((4,)),
             dma((4,)),
             dma((CHUNKS,)),

time: 81.2 us -> 80.7 us (level)
  no operation moved by 1% of the time
where the time goes in v4:
time: 80.7 us; the launch traced here: 80.5 us
  Pallas kernels  79.9 us (99%)
    pallas_call x1, Pallas kernels, shards_step(): pl.pallas_call(functools.partial(kernel, sizes), name='shampoo', out_shap...  77.4 us
    pallas_call x1, Pallas kernels, shards_step(): pl.pallas_call(functools.partial(hand_over, len(outs)), name='hand_over',...  2.54 us

profile of v4, /device:TPU:1, one launch (start us, length us, event | category | flops | bytes accessed | tf_op | source)
XLA Modules:
  0.0 80.5 jit_solution(1732705515431578953)
XLA Ops:
  0.6 77.4 %shampoo.1 = (bf16[8,64,4,256]{3,2,1,0:T(4,128)(2,1)}, f32[2,256,256]{2,1,0:T(8,128)}, f32[2,256,256]{2,1,0:T(8,128)}) custom-call(s32[1,64]{1,0:T(1,128)} %bitcast.1, bf16[8,64,4,256]{3,2,1,0:T(4,128)(2,1)} %x_hbm.1, bf16[2,256,256]{2,1,0:T(8,128)(2,1)} %left_hbm.1, bf16[2,256,256]{2,1,0:T(8,128)(2,1)} %right_hbm.1, f32[2,256,256]{2,1,0:T(8,128)} %left_old_hbm.1, ...), custom_call_target="tpu_custom_call" | custom-call | tf_op jit(solution)/shard_map/shampoo/pallas_call | solution.py:599
  78.0 2.5 %hand_over.1 = (bf16[8,64,4,256]{3,2,1,0:T(4,128)(2,1)}, f32[2,256,256]{2,1,0:T(8,128)}, f32[2,256,256]{2,1,0:T(8,128)}) custom-call(bf16[8,64,4,256]{3,2,1,0:T(4,128)(2,1)} %get-tuple-element.6.refs_0_, f32[2,256,256]{2,1,0:T(8,128)} %get-tuple-element.7.refs_1_, f32[2,256,256]{2,1,0:T(8,128)} %get-tuple-element.8.refs_2_), custom_call_target="tpu_custom_call" | custom-call | tf_op jit(solution)/shard_map/hand_over/pallas_call | solution.py:661

commit v5 on v4

--- a/solution.py
+++ b/solution.py
@@ -457,7 +457,10 @@
             ).start()
             return carry
 
-        lax.fori_loop(1, holders, send, 0)
+        lax.fori_loop(1, holders // 2, send, 0)
+        if c == CHUNKS - 1:
+            pass_tiles(grams_b, grams_c, grams_d, 3, 3)
+        lax.fori_loop(holders // 2, holders, send, 0)
         back[c][me] = back_stage[c, me]
 
     left_new[0] = jnp.zeros((width, width), jnp.float32)
@@ -508,8 +511,6 @@
         loads[4 + side].wait()
         new[0] = jnp.where(load > 0, kept * old[0] + new[0], old[0])
         store(new.at[0], target.at[0])
-
-    pass_tiles(grams_b, grams_c, grams_d, 3, 3)
 
     def finish(c):
         wait_bytes(back[c], holders - 1, recv_back.at[c])

time: 80.7 us -> 80.9 us (level)
  no operation moved by 1% of the time
where the time goes in v5:
time: 80.9 us; the launch traced here: 80.7 us
  Pallas kernels  80.1 us (99%)
    pallas_call x1, Pallas kernels, shards_step(): pl.pallas_call(functools.partial(kernel, sizes), name='shampoo', out_shap...  77.5 us
    pallas_call x1, Pallas kernels, shards_step(): pl.pallas_call(functools.partial(hand_over, len(outs)), name='hand_over',...  2.54 us

profile of v5, /device:TPU:1, one launch (start us, length us, event | category | flops | bytes accessed | tf_op | source)
XLA Modules:
  0.0 80.7 jit_solution(15916974077489260334)
XLA Ops:
  0.6 77.5 %shampoo.1 = (bf16[8,64,4,256]{3,2,1,0:T(4,128)(2,1)}, f32[2,256,256]{2,1,0:T(8,128)}, f32[2,256,256]{2,1,0:T(8,128)}) custom-call(s32[1,64]{1,0:T(1,128)} %bitcast.1, bf16[8,64,4,256]{3,2,1,0:T(4,128)(2,1)} %x_hbm.1, bf16[2,256,256]{2,1,0:T(8,128)(2,1)} %left_hbm.1, bf16[2,256,256]{2,1,0:T(8,128)(2,1)} %right_hbm.1, f32[2,256,256]{2,1,0:T(8,128)} %left_old_hbm.1, ...), custom_call_target="tpu_custom_call" | custom-call | tf_op jit(solution)/shard_map/shampoo/pallas_call | solution.py:600
  78.2 2.5 %hand_over.1 = (bf16[8,64,4,256]{3,2,1,0:T(4,128)(2,1)}, f32[2,256,256]{2,1,0:T(8,128)}, f32[2,256,256]{2,1,0:T(8,128)}) custom-call(bf16[8,64,4,256]{3,2,1,0:T(4,128)(2,1)} %get-tuple-element.6.refs_0_, f32[2,256,256]{2,1,0:T(8,128)} %get-tuple-element.7.refs_1_, f32[2,256,256]{2,1,0:T(8,128)} %get-tuple-element.8.refs_2_), custom_call_target="tpu_custom_call" | custom-call | tf_op jit(solution)/shard_map/hand_over/pallas_call | solution.py:662

commit v6 on v5

--- a/solution.py
+++ b/solution.py
@@ -217,7 +217,7 @@
             axis=0,
         )
 
-    carries = lax.rem(me, 2) == 0
+    carries = lax.rem(me, 2) == lax.rem(me // 2, 2)
     mine = me // 2
     homes = (1, holders // 2 + 1)
     holds = (me == homes[0]) | (me == homes[1])
@@ -281,7 +281,7 @@
             up = jnp.where(far, i % 7 + 1, 0)
             along = jnp.where(far, i // 7, i - 7 * chips)
             chip = (me // plane + up) % 8 * chips + (me // 2 + along) % chips
-            tile, d = chip, 2 * chip
+            tile, d = chip, 2 * chip + chip % 2
 
             @pl.when(d != me)
             def _():

time: 80.9 us -> 81.8 us (1.011); the launches traced: 80.7 us -> 80.7 us
  no operation moved by 1% of the time
where the time goes in v6:
time: 81.8 us; the launch traced here: 80.7 us
  Pallas kernels  80.1 us (98%)
    pallas_call x1, Pallas kernels, shards_step(): pl.pallas_call(functools.partial(kernel, sizes), name='shampoo', out_shap...  77.6 us
    pallas_call x1, Pallas kernels, shards_step(): pl.pallas_call(functools.partial(hand_over, len(outs)), name='hand_over',...  2.54 us

profile of v6, /device:TPU:1, one launch (start us, length us, event | category | flops | bytes accessed | tf_op | source)
XLA Modules:
  0.0 80.7 jit_solution(7136916556084761103)
XLA Ops:
  0.6 77.6 %shampoo.1 = (bf16[8,64,4,256]{3,2,1,0:T(4,128)(2,1)}, f32[2,256,256]{2,1,0:T(8,128)}, f32[2,256,256]{2,1,0:T(8,128)}) custom-call(s32[1,64]{1,0:T(1,128)} %bitcast.1, bf16[8,64,4,256]{3,2,1,0:T(4,128)(2,1)} %x_hbm.1, bf16[2,256,256]{2,1,0:T(8,128)(2,1)} %left_hbm.1, bf16[2,256,256]{2,1,0:T(8,128)(2,1)} %right_hbm.1, f32[2,256,256]{2,1,0:T(8,128)} %left_old_hbm.1, ...), custom_call_target="tpu_custom_call" | custom-call | tf_op jit(solution)/shard_map/shampoo/pallas_call | solution.py:600
  78.2 2.5 %hand_over.1 = (bf16[8,64,4,256]{3,2,1,0:T(4,128)(2,1)}, f32[2,256,256]{2,1,0:T(8,128)}, f32[2,256,256]{2,1,0:T(8,128)}) custom-call(bf16[8,64,4,256]{3,2,1,0:T(4,128)(2,1)} %get-tuple-element.6.refs_0_, f32[2,256,256]{2,1,0:T(8,128)} %get-tuple-element.7.refs_1_, f32[2,256,256]{2,1,0:T(8,128)} %get-tuple-element.8.refs_2_), custom_call_target="tpu_custom_call" | custom-call | tf_op jit(solution)/shard_map/hand_over/pallas_call | solution.py:662
